TPU v7x, 32 devices: a whole 2x2x4 slice. The times are simulated.
32 devices in a mesh: dp: 16 (over z, x, core), seq: 2 (over y).
Axes of the slice: x: 2, y: 2, z: 4, core: 2. Of those that a mesh axis runs over, the one named last changes fastest.
Arguments:
- tokens: bfloat16 [32, 1024, 768], P('dp', 'seq'), may hold values from -6 to 6
- first_values: bfloat16 [32, 1024, 384], P('dp', 'seq'), may hold values from -6 to 6
- cotangent: bfloat16 [32, 1024, 768], P('dp', 'seq'), may hold values from -6 to 6
- lengths: int32 [32], P('dp'), may hold values from 256 to 1024, as said below
- qkv_master: float32 [768, 1920], P(('dp', 'seq')), may hold values from -0.21875 to 0.21875
- qkv_moment: float32 [768, 1920], P(('dp', 'seq')), may hold values from -112 to 112
- qkv_average: float32 [768, 1920], P(('dp', 'seq')), may hold values from -0.21875 to 0.21875
- out_master: float32 [768, 768], P(('dp', 'seq')), may hold values from -1.75 to 1.75
- out_moment: float32 [768, 768], P(('dp', 'seq')), may hold values from -224 to 224
- out_average: float32 [768, 768], P(('dp', 'seq')), may hold values from -1.75 to 1.75
- up_master: float32 [768, 3072], P(('dp', 'seq')), may hold values from -0.21875 to 0.21875
- up_moment: float32 [768, 3072], P(('dp', 'seq')), may hold values from -448 to 448
- up_average: float32 [768, 3072], P(('dp', 'seq')), may hold values from -0.21875 to 0.21875
- down_master: float32 [3072, 768], P(('dp', 'seq')), may hold values from -0.109375 to 0.109375
- down_moment: float32 [3072, 768], P(('dp', 'seq')), may hold values from -448 to 448
- down_average: float32 [3072, 768], P(('dp', 'seq')), may hold values from -0.109375 to 0.109375
- norm_master: float32 [768, 4], P(('dp', 'seq')), may hold values from -0.5 to 1.4, as said below
- norm_moment: float32 [768, 4], P(('dp', 'seq')), may hold values from -512 to 512
- norm_average: float32 [768, 4], P(('dp', 'seq')), may hold values from -6 to 6
Outputs:
- mixed: bfloat16 [32, 1024, 768], P('dp', 'seq')
- tokens_grad: bfloat16 [32, 1024, 768], P('dp', 'seq')
- first_values_grad: bfloat16 [32, 1024, 384], P('dp', 'seq')
- qkv_moment_new: float32 [768, 1920], P(('dp', 'seq'))
- qkv_master_new: float32 [768, 1920], P(('dp', 'seq'))
- qkv_average_new: float32 [768, 1920], P(('dp', 'seq'))
- out_moment_new: float32 [768, 768], P(('dp', 'seq'))
- out_master_new: float32 [768, 768], P(('dp', 'seq'))
- out_average_new: float32 [768, 768], P(('dp', 'seq'))
- up_moment_new: float32 [768, 3072], P(('dp', 'seq'))
- up_master_new: float32 [768, 3072], P(('dp', 'seq'))
- up_average_new: float32 [768, 3072], P(('dp', 'seq'))
- down_moment_new: float32 [3072, 768], P(('dp', 'seq'))
- down_master_new: float32 [3072, 768], P(('dp', 'seq'))
- down_average_new: float32 [3072, 768], P(('dp', 'seq'))
- norm_moment_new: float32 [768, 4], P(('dp', 'seq'))
- norm_master_new: float32 [768, 4], P(('dp', 'seq'))
- norm_average_new: float32 [768, 4], P(('dp', 'seq'))
Inputs may be any that keep to these rules, and one draw needn't show every extreme that they name: `lengths`: in every draw some sequence has all 1024 positions. `norm_master`: columns 0 and 2 are gains, columns 1 and 3 shifts.
All inputs are finite; a program needn't handle non-finite values.
Results may differ from a plain program's by a relative error of at most 0.012.
Values may be sent and summed in bfloat16 or wider, within the bound.
No kernel may reach another device: no remote copies, remote signals or barrier semaphores. Data moves between devices by JAX's collectives and lax.ppermute only.
A program may use at most 192 MiB of HBM per device.

v0:
```python
import jax
import jax.numpy as jnp
from jax import lax
from jax.sharding import PartitionSpec as P

HEAD_DIM = 64


EPSILON = 1e-05
MOMENTUM = 0.5
AVERAGING = 0.5
RATE = 0.0006


def layer_norm(values, gain, shift):
    center = values - jnp.mean(values, -1, keepdims=True)
    spread = jnp.mean(center * center, -1, keepdims=True)
    return center * lax.rsqrt(spread + EPSILON) * gain + shift


def gelu_tanh(values):
    return jax.nn.gelu(values, approximate=True)


def contract_rows(left, right):
    return lax.dot_general(
        left, right, (((0,), (0,)), ((), ())), preferred_element_type=jnp.float32
    )


def times_transposed(left, right):
    return lax.dot_general(
        left, right, (((1,), (1,)), ((), ())), preferred_element_type=jnp.float32
    )


def block_scores(query_block, key_heads, start):
    scores = jnp.einsum(
        "qhd,khd->hqk", query_block, key_heads, preferred_element_type=jnp.float32
    ) * HEAD_DIM ** (-0.5)
    row_index = start + lax.iota(jnp.int32, query_block.shape[0])
    column_index = lax.iota(jnp.int32, key_heads.shape[0])
    visible = row_index[:, None] >= column_index[None, :]
    return jnp.where(visible[None], scores, -1e30)


def split_blocks(values):
    length = values.shape[0]
    block_rows = min(512, length)
    block_count = length // block_rows
    starts = lax.iota(jnp.int32, block_count) * block_rows
    return (values.reshape((block_count, block_rows) + values.shape[1:]), starts)


def attend_forward(query_heads, key_heads, value_heads):
    query_blocks, starts = split_blocks(query_heads)

    def one_block(block_args):
        query_block, start = block_args
        scores = block_scores(query_block, key_heads, start)
        maximum = jnp.max(scores, -1, keepdims=True)
        weights = jnp.exp(scores - maximum)
        summed = jnp.sum(weights, -1, keepdims=True)
        probs = (weights / summed).astype(jnp.bfloat16)
        output = jnp.einsum("hqk,khd->qhd", probs, value_heads, preferred_element_type=jnp.float32)
        return (output.astype(jnp.bfloat16), (maximum + jnp.log(summed))[..., 0])

    outputs, log_totals = lax.map(one_block, (query_blocks, starts))
    return (outputs.reshape(query_heads.shape), log_totals)


def attend_backward(query_heads, key_heads, value_heads, grad_heads, log_totals):
    query_blocks, starts = split_blocks(query_heads)
    grad_blocks, unused_starts = split_blocks(grad_heads)
    score_scale = HEAD_DIM ** (-0.5)

    def one_block(carry, block_args):
        grad_keys, grad_values = carry
        query_block, grad_block, block_totals, start = block_args
        scores = block_scores(query_block, key_heads, start)
        probs = jnp.exp(scores - block_totals[..., None])
        grad_probs = jnp.einsum(
            "qhd,khd->hqk", grad_block, value_heads, preferred_element_type=jnp.float32
        )
        inner = jnp.sum(probs * grad_probs, -1, keepdims=True)
        grad_scores = (probs * (grad_probs - inner)).astype(jnp.bfloat16)
        grad_query = (
            jnp.einsum("hqk,khd->qhd", grad_scores, key_heads, preferred_element_type=jnp.float32)
            * score_scale
        )
        grad_keys = (
            grad_keys
            + jnp.einsum(
                "hqk,qhd->khd", grad_scores, query_block, preferred_element_type=jnp.float32
            )
            * score_scale
        )
        grad_values = grad_values + jnp.einsum(
            "hqk,qhd->khd",
            probs.astype(jnp.bfloat16),
            grad_block,
            preferred_element_type=jnp.float32,
        )
        return ((grad_keys, grad_values), grad_query)

    zeros = jnp.zeros(key_heads.shape, jnp.float32)
    (grad_keys, grad_values), grad_query = lax.scan(
        one_block, (zeros, zeros), (query_blocks, grad_blocks, log_totals, starts)
    )
    return (grad_query.reshape(query_heads.shape), grad_keys, grad_values)


def update(gradient, moment, master, average):
    moment_new = MOMENTUM * moment + gradient
    master_new = master - RATE * (gradient + MOMENTUM * moment_new)
    average_new = AVERAGING * average + (1.0 - AVERAGING) * master_new
    return (moment_new, master_new, average_new)


def body(
    tokens,
    first_values,
    cotangent,
    lengths,
    qkv_master,
    qkv_moment,
    qkv_average,
    out_master,
    out_moment,
    out_average,
    up_master,
    up_moment,
    up_average,
    down_master,
    down_moment,
    down_average,
    norm_master,
    norm_moment,
    norm_average,
):
    seq_count, half_len, model_width = tokens.shape
    row_count = seq_count * half_len
    w_qkv, w_out, norm_work, w_up, w_down = (
        lax.all_gather(qkv_master.astype(jnp.bfloat16), ("dp", "seq"), axis=0, tiled=True),
        lax.all_gather(out_master.astype(jnp.bfloat16), ("dp", "seq"), axis=0, tiled=True),
        lax.all_gather(norm_master.astype(jnp.bfloat16), ("dp", "seq"), axis=0, tiled=True),
        lax.all_gather(up_master.astype(jnp.bfloat16), ("dp", "seq"), axis=0, tiled=True),
        lax.all_gather(down_master.astype(jnp.bfloat16), ("dp", "seq"), axis=0, tiled=True),
    )
    norm_param = norm_work.astype(jnp.float32)
    rows_in = tokens.astype(jnp.float32).reshape(row_count, model_width)
    normed_one, pull_one = jax.vjp(layer_norm, rows_in, norm_param[:, 0], norm_param[:, 1])
    normed_one = normed_one.astype(jnp.bfloat16)
    projected = jnp.dot(normed_one, w_qkv, preferred_element_type=jnp.float32)
    values_all = jnp.concatenate(
        [
            projected[:, 2 * model_width :].astype(jnp.bfloat16),
            first_values.reshape(row_count, model_width // 2),
        ],
        1,
    )
    stacked = jnp.stack(
        [
            projected[:, :model_width].astype(jnp.bfloat16),
            projected[:, model_width : 2 * model_width].astype(jnp.bfloat16),
            values_all,
        ]
    ).reshape(3, seq_count, half_len, model_width)
    head_layout = lax.all_to_all(stacked, "seq", split_axis=3, concat_axis=2, tiled=True)
    seq_len = head_layout.shape[2]
    head_width = head_layout.shape[3]
    head_count = head_width // HEAD_DIM
    split_heads = head_layout.reshape(3, seq_count, seq_len, head_count, HEAD_DIM)

    def forward_seq(seq_args):
        return attend_forward(seq_args[0], seq_args[1], seq_args[2])

    attended, log_totals = lax.map(forward_seq, (split_heads[0], split_heads[1], split_heads[2]))
    token_layout = lax.all_to_all(
        attended.reshape(seq_count, seq_len, head_width),
        "seq",
        split_axis=1,
        concat_axis=2,
        tiled=True,
    )
    attended_rows = token_layout.reshape(row_count, model_width)
    mid_rows = rows_in + jnp.dot(attended_rows, w_out, preferred_element_type=jnp.float32)
    normed_two, pull_two = jax.vjp(layer_norm, mid_rows, norm_param[:, 2], norm_param[:, 3])
    normed_two = normed_two.astype(jnp.bfloat16)
    hidden_pre = jnp.dot(normed_two, w_up, preferred_element_type=jnp.float32)
    hidden, pull_gelu = jax.vjp(gelu_tanh, hidden_pre)
    hidden = hidden.astype(jnp.bfloat16)
    mixed = (
        (mid_rows + jnp.dot(hidden, w_down, preferred_element_type=jnp.float32))
        .astype(jnp.bfloat16)
        .reshape(tokens.shape)
    )
    position = lax.axis_index("seq") * half_len + lax.iota(jnp.int32, half_len)
    keep_mask = position[None, :] < lengths[:, None]
    grad_mixed = jnp.where(keep_mask[:, :, None], cotangent, jnp.zeros_like(cotangent)).reshape(
        row_count, model_width
    )
    grad_down = contract_rows(hidden, grad_mixed)
    grad_hidden = pull_gelu(times_transposed(grad_mixed, w_down))[0].astype(jnp.bfloat16)
    grad_up = contract_rows(normed_two, grad_hidden)
    grad_mid_norm, grad_gain_two, grad_shift_two = pull_two(times_transposed(grad_hidden, w_up))
    grad_mid = grad_mixed.astype(jnp.float32) + grad_mid_norm
    grad_mid_low = grad_mid.astype(jnp.bfloat16)
    grad_out = contract_rows(attended_rows, grad_mid_low)
    grad_attended = (
        times_transposed(grad_mid_low, w_out)
        .astype(jnp.bfloat16)
        .reshape(seq_count, half_len, model_width)
    )
    grad_heads = lax.all_to_all(grad_attended, "seq", split_axis=2, concat_axis=1, tiled=True)

    def backward_seq(seq_args):
        return attend_backward(seq_args[0], seq_args[1], seq_args[2], seq_args[3], seq_args[4])

    grad_query, grad_keys, grad_values = lax.map(
        backward_seq,
        (
            split_heads[0],
            split_heads[1],
            split_heads[2],
            grad_heads.reshape(seq_count, seq_len, head_count, HEAD_DIM),
            log_totals,
        ),
    )
    stacked_grads = (
        jnp.stack([grad_query, grad_keys, grad_values])
        .astype(jnp.bfloat16)
        .reshape(3, seq_count, seq_len, head_width)
    )
    token_grads = lax.all_to_all(
        stacked_grads, "seq", split_axis=2, concat_axis=3, tiled=True
    ).reshape(3, row_count, model_width)
    grad_columns = jnp.concatenate(
        [token_grads[0], token_grads[1], token_grads[2][:, : model_width // 2]], 1
    )
    grad_qkv = contract_rows(normed_one, grad_columns)
    grad_in_norm, grad_gain_one, grad_shift_one = pull_one(times_transposed(grad_columns, w_qkv))
    tokens_grad = (grad_mid + grad_in_norm).astype(jnp.bfloat16).reshape(tokens.shape)
    first_grad = token_grads[2][:, model_width // 2 :].reshape(first_values.shape)
    sum_qkv, sum_out, sum_up, sum_down, sum_norm = (
        lax.psum_scatter(grad_qkv, ("dp", "seq"), scatter_dimension=0, tiled=True),
        lax.psum_scatter(grad_out, ("dp", "seq"), scatter_dimension=0, tiled=True),
        lax.psum_scatter(grad_up, ("dp", "seq"), scatter_dimension=0, tiled=True),
        lax.psum_scatter(grad_down, ("dp", "seq"), scatter_dimension=0, tiled=True),
        lax.psum_scatter(
            jnp.stack([grad_gain_one, grad_shift_one, grad_gain_two, grad_shift_two], 1),
            ("dp", "seq"),
            scatter_dimension=0,
            tiled=True,
        ),
    )
    qkv_new = update(sum_qkv, qkv_moment, qkv_master, qkv_average)
    out_new = update(sum_out, out_moment, out_master, out_average)
    up_new = update(sum_up, up_moment, up_master, up_average)
    down_new = update(sum_down, down_moment, down_master, down_average)
    norm_new = update(sum_norm, norm_moment, norm_master, norm_average)
    return (
        mixed,
        tokens_grad,
        first_grad,
        qkv_new[0],
        qkv_new[1],
        qkv_new[2],
        out_new[0],
        out_new[1],
        out_new[2],
        up_new[0],
        up_new[1],
        up_new[2],
        down_new[0],
        down_new[1],
        down_new[2],
        norm_new[0],
        norm_new[1],
        norm_new[2],
    )


def solution(mesh):
    in_specs = (
        P("dp", "seq", None),
        P("dp", "seq", None),
        P("dp", "seq", None),
        P("dp"),
        P(("dp", "seq"), None),
        P(("dp", "seq"), None),
        P(("dp", "seq"), None),
        P(("dp", "seq"), None),
        P(("dp", "seq"), None),
        P(("dp", "seq"), None),
        P(("dp", "seq"), None),
        P(("dp", "seq"), None),
        P(("dp", "seq"), None),
        P(("dp", "seq"), None),
        P(("dp", "seq"), None),
        P(("dp", "seq"), None),
        P(("dp", "seq"), None),
        P(("dp", "seq"), None),
        P(("dp", "seq"), None),
    )
    out_specs = (
        P("dp", "seq", None),
        P("dp", "seq", None),
        P("dp", "seq", None),
        P(("dp", "seq"), None),
        P(("dp", "seq"), None),
        P(("dp", "seq"), None),
        P(("dp", "seq"), None),
        P(("dp", "seq"), None),
        P(("dp", "seq"), None),
        P(("dp", "seq"), None),
        P(("dp", "seq"), None),
        P(("dp", "seq"), None),
        P(("dp", "seq"), None),
        P(("dp", "seq"), None),
        P(("dp", "seq"), None),
        P(("dp", "seq"), None),
        P(("dp", "seq"), None),
        P(("dp", "seq"), None),
    )
    return jax.shard_map(body, mesh=mesh, in_specs=in_specs, out_specs=out_specs, check_vma=False)
```

profile of v0, /device:TPU:0, one launch (start us, length us, event | category | flops | bytes accessed | tf_op | source)
XLA Modules:
  0.0 1113.4 jit_solution(2314486756077897497)
XLA Ops:
  13.4 69.8 %all-gather = bf16[32,24,4]{1,2,0:T(4,128)(2,1)S(1)} all-gather(bf16[1,24,4]{1,2,0:T(4,128)(2,1)S(1)} %convert_bitcast_fusion), channel_id=1, replica_groups=mesh['dp'=16,'seq'=2] {'dp','seq'}, dimensions={0}, use_global_device_ids=true | all-gather | bytes 6336 | tf_op jit(solution)/shard_map/all_gather | solution.py:146
  87.2 6.0 convolution_convert_fusion
  103.7 13.7 %maximum_maximum_fusion = bf16[3,2,512,768]{2,1,0,3:T(2,128)(2,1)} fusion(bf16[1,2,512,384]{2,1,0,3:T(2,128)(2,1)} %bitcast.252, bf16[1,2,512,384]{2,1,0,3:T(2,128)(2,1)} %copy.103, bf16[1,2,512,768]{2,1,0,3:T(2,128)(2,1)S(1)} %copy.105, bf16[1,2,512,768]{2,1,0,3:T(2,128)(2,1)S(1)} %copy.104), kind=kLoop, calls=%fused_computation.75 | loop fusion | flops 7077888 | bytes 9437184 | tf_op jit(solution)/shard_map/stack | solution.py:162
  117.4 5.9 all-to-all-start
  124.9 51.9 %all-to-all-done = bf16[3,2,512,768]{2,1,0,3:T(2,128)(2,1)} async-done(((bf16[3,2,512,768]{2,1,0,3:T(2,128)(2,1)}), bf16[3,2,512,768]{2,1,0,3:T(2,128)(2,1)}, u32[]{:S(2)}, u32[]{:S(2)}) %all-to-all-start) | async-done | bytes 4718624 | tf_op jit(solution)/shard_map/all_to_all | solution.py:169
  176.8 9.3 copy.145
  186.1 6.4 fusion.67
  200.9 65.0 %while.54 = (s32[]{:T(128)}, bf16[2,1024,6,64]{1,3,2,0:T(8,128)(2,1)}, f32[2,2,6,512]{3,2,1,0:T(8,128)S(1)}, bf16[2,1024,6,64]{1,3,2,0:T(8,128)(2,1)}, bf16[2,10...) while((s32[]{:T(128)}, ...), condition=%wide.region_7.8_spmd, body=%wide.region_2.7_spmd.sunk | while | flops 843773440 | bytes 58122584 | solution.py:178
  205.3 24.3 %while.57 = (s32[]{:T(128)}, bf16[2,512,6,64]{1,3,2,0:T(8,128)(2,1)S(1)}, f32[2,6,512]{2,1,0:T(8,128)S(1)}, s32[2]{0:T(128)S(1)}, bf16[2,512,6,64]{1,3,2,0:T(8,1...) while((s32[]{:T(128)}, ...), condition=%wide.region_6.6_spmd, body=%wide.region_3.5_spmd.sunk | while | flops 843773440 | bytes 45473940 | solution.py:68
  212.9 4.4 fusion.128
  225.1 4.4 fusion.128
  237.7 24.3 %while.57 = (s32[]{:T(128)}, bf16[2,512,6,64]{1,3,2,0:T(8,128)(2,1)S(1)}, f32[2,6,512]{2,1,0:T(8,128)S(1)}, s32[2]{0:T(128)S(1)}, bf16[2,512,6,64]{1,3,2,0:T(8,1...) while((s32[]{:T(128)}, ...), condition=%wide.region_6.6_spmd, body=%wide.region_3.5_spmd.sunk | while | flops 843773440 | bytes 45473940 | solution.py:68
  245.4 4.4 fusion.128
  257.6 4.4 fusion.128
  265.9 5.0 copy.108
  276.6 13.8 %all-to-all-done.1 = bf16[2,1024,384]{2,0,1:T(2,128)(2,1)S(1)} async-done(((bf16[2,1024,384]{2,0,1:T(2,128)(2,1)}), bf16[2,1024,384]{2,0,1:T(2,128)(2,1)S(1)}, u32[]{:S(2)}, u32[]{:S(2)}) %all-to-all-start.1) | async-done | bytes 1572896 | tf_op jit(solution)/shard_map/all_to_all | solution.py:179
  301.7 8.2 fusion.63
  309.9 4.5 copy-done.71
  314.4 9.2 fusion.64
  323.7 131.8 %reduce-scatter.12.cloned.1.call-done = f32[96,768]{1,0:T(8,128)} async-done(((f32[3072,768]{1,0:T(8,128)}), f32[96,768]{1,0:T(8,128)}) %reduce-scatter.12.cloned.1.call-update) | async-done | bytes 294928 | tf_op jit(solution)/shard_map/reduce_scatter | solution.py:249
  457.5 64.4 %all-gather.12.cloned.1.call-done = bf16[3072,768]{1,0:T(8,128)(2,1)} async-done(((bf16[96,768]{1,0:T(8,128)(2,1)}), bf16[3072,768]{1,0:T(8,128)(2,1)}) %all-gather.12.cloned.1.call-update) | async-done | bytes 4718608 | tf_op jit(solution)/shard_map/all_gather | solution.py:148
  521.9 15.8 %fusion.42 = bf16[1024,3072]{1,0:T(8,128)(2,1)S(1)} fusion(f32[1024,3072]{1,0:T(8,128)} %copy-done.71, bf16[1024,768]{1,0:T(8,128)(2,1)} %bitcast.242, bf16[3072,768]{1,0:T(8,128)(2,1)} %all-gather.12.cloned.1.call-done), kind=kOutput, calls=%fused_computation.71 | convolution fusion | flops 4894752768 | bytes 25165824 | tf_op jit(solution)/shard_map/dot_general | solution.py:32
  537.7 10.8 multiply_reduce_fusion.1
  560.4 19.9 %all-to-all-done.2 = bf16[2,512,768]{1,0,2:T(2,128)(2,1)S(1)} async-done(((bf16[2,512,768]{1,0,2:T(2,128)(2,1)}), bf16[2,512,768]{1,0,2:T(2,128)(2,1)S(1)}, u32[]{:S(2)}, u32[]{:S(2)}) %all-to-all-start.2) | async-done | bytes 1572896 | tf_op jit(solution)/shard_map/all_to_all | solution.py:215
  584.5 132.1 %while.56 = (s32[]{:T(128)}, bf16[2,1024,6,64]{1,3,2,0:T(8,128)(2,1)}, bf16[2,1024,6,64]{1,3,2,0:T(8,128)(2,1)}, bf16[2,1024,6,64]{1,3,2,0:T(8,128)(2,1)}, bf16[...) while((s32[]{:T(128)}, ...), condition=%wide.region_16.17_spmd, body=%wide.region_12.16_spmd.sunk | while | flops 2063136256 | bytes 163070640 | solution.py:220
  591.7 49.2 %while.58 = (s32[]{:T(128)}, f32[1024,6,64]{0,2,1:T(8,128)S(1)}, f32[1024,6,64]{0,2,1:T(8,128)}, bf16[2,512,6,64]{1,3,2,0:T(8,128)(2,1)}, bf16[2,512,6,64]{1,3,2...) while((s32[]{:T(128)}, f32[1024,6,64]{0,2,1:T(8,128)S(1)}, ...), condition=%wide.region_15.15_spmd.clone, body=%wide.region_13.14_spmd.clone.sunk | while | flops 2063136256 | bytes 132743520 | solution.py:107
  598.8 7.2 multiply_reduce_fusion.5
  606.0 6.9 multiply_convert_fusion.5
  623.4 7.2 multiply_reduce_fusion.5
  630.6 6.9 multiply_convert_fusion.5
  657.5 49.2 %while.58 = (s32[]{:T(128)}, f32[1024,6,64]{0,2,1:T(8,128)S(1)}, f32[1024,6,64]{0,2,1:T(8,128)}, bf16[2,512,6,64]{1,3,2,0:T(8,128)(2,1)}, bf16[2,512,6,64]{1,3,2...) while((s32[]{:T(128)}, f32[1024,6,64]{0,2,1:T(8,128)S(1)}, ...), condition=%wide.region_15.15_spmd.clone, body=%wide.region_13.14_spmd.clone.sunk | while | flops 2063136256 | bytes 132743520 | solution.py:107
  664.6 7.2 multiply_reduce_fusion.5
  671.8 6.9 multiply_convert_fusion.5
  689.2 7.2 multiply_reduce_fusion.5
  696.4 6.9 multiply_convert_fusion.5
  716.6 5.1 pad_maximum_fusion
  721.7 12.6 %copy.116 = bf16[3,2,1024,384]{3,1,0,2:T(2,128)(2,1)} copy(bf16[3,2,1024,384]{2,3,1,0:T(8,128)(2,1)} %pad_maximum_fusion) | data formatting | bytes 9437184 | tf_op jit(solution)/shard_map/stack | solution.py:231
  734.3 6.1 all-to-all-start.3
  743.3 49.9 %all-to-all-done.3 = bf16[3,2,1024,384]{3,1,0,2:T(2,128)(2,1)} async-done(((bf16[3,2,1024,384]{3,1,0,2:T(2,128)(2,1)}), bf16[3,2,1024,384]{3,1,0,2:T(2,128)(2,1)}, u32[]{:S(2)}, u32[]{:S(2)}) %all-to-all-start.3) | async-done | bytes 4718624 | tf_op jit(solution)/shard_map/all_to_all | solution.py:235
  793.2 9.5 copy.144
  802.8 4.9 fusion.66
  810.9 5.6 fusion.55
  818.4 10.7 fusion.62
  829.9 13.2 %add_convert_fusion.1 = bf16[1024,768]{1,0:T(8,128)(2,1)} fusion(f32[1024,768]{1,0:T(8,128)} %copy-done.7, bf16[3072,768]{1,0:T(8,128)(2,1)} %all-gather.12.cloned.1.call-done, f32[1024,3072]{1,0:T(8,128)} %copy-done.71), kind=kOutput, calls=%fused_computation.100 | convolution fusion | flops 4861722624 | bytes 22020096 | tf_op jit(solution)/shard_map/dot_general | solution.py:194
  850.4 39.8 %all-reduce.1 = f32[768,4]{0,1:T(4,128)S(1)} all-reduce(f32[768,4]{0,1:T(4,128)S(1)} %pad_maximum_fusion.4), channel_id=6, replica_groups=mesh['dp'=16,'seq'=2] {'dp','seq'}, use_global_device_ids=true, to_apply=%region_27.28.clone | all-reduce | flops 3072 | bytes 24576
  892.5 4.5 add_convert_fusion
  897.0 66.6 %reduce-scatter.14.cloned.1.call-done = f32[24,1920]{1,0:T(8,128)} async-done(((f32[768,1920]{1,0:T(8,128)}), f32[24,1920]{1,0:T(8,128)}) %reduce-scatter.14.cloned.1.call-update) | async-done | bytes 184336
  965.7 138.6 %reduce-scatter.10.cloned.1.call-done = f32[24,3072]{1,0:T(8,128)} async-done(((f32[768,3072]{1,0:T(8,128)}), f32[24,3072]{1,0:T(8,128)}) %reduce-scatter.10.cloned.1.call-update) | async-done | bytes 294928 | tf_op jit(solution)/shard_map/reduce_scatter | solution.py:248
  (392 shorter events, 208.8 us)
Async XLA Ops:
  7.2 79.3 %copy-start.2 = (bf16[2,512,768]{2,1,0:T(8,128)(2,1)S(1)}, bf16[2,512,768]{2,1,0:T(8,128)(2,1)}, u32[]{:S(2)}) copy-start(bf16[2,512,768]{2,1,0:T(8,128)(2,1)} %param.27) | copy-start | bytes 4718596
  7.2 76.2 %copy-start.32 = (bf16[2,512,384]{2,1,0:T(8,128)(2,1)S(1)}, bf16[2,512,384]{2,1,0:T(8,128)(2,1)}, u32[]{:S(2)}) copy-start(bf16[2,512,384]{2,1,0:T(8,128)(2,1)} %param.28) | copy-start | bytes 2359300
  7.2 80.0 %all-gather.6.cloned.1.call-start = ((), (), s32[]{:S(2)}) async-start(), calls=%async_computation.8 | async-start | bytes 3041280 | tf_op jit(solution)/shard_map/all_gather | solution.py:144
  10.7 76.4 %copy-start.54 = (f32[1,4,2,128]{3,1,2,0:T(4,128)}, f32[1,4,2,128]{3,1,2,0:T(4,128)S(1)}, u32[]{:S(2)}) copy-start(f32[1,4,2,128]{3,1,2,0:T(4,128)S(1)} %copy.136) | copy-start | bytes 12292
  13.4 79.8 %copy-start.56 = (f32[1024]{0:T(1024)}, f32[1024]{0:T(1024)S(1)}, u32[]{:S(2)}) copy-start(f32[1024]{0:T(1024)S(1)} %rsqrt.20) | copy-start | bytes 12292
  117.4 59.4 %all-to-all-start = ((bf16[3,2,512,768]{2,1,0,3:T(2,128)(2,1)}), bf16[3,2,512,768]{2,1,0,3:T(2,128)(2,1)}, u32[]{:S(2)}, u32[]{:S(2)}) async-start(bf16[3,2,512,768]{2,1,0,3:T(2,128)(2,1)} %maximum_maximum_fusion), calls=%async_computation | async-start | bytes 9437184 | tf_op jit(solution)/shard_map/all_to_all | solution.py:169
  123.4 172.8 %all-gather.8.cloned.1.call-start = ((), (), s32[]{:S(2)}) async-start(), calls=%async_computation.9 | async-start | bytes 1216512 | tf_op jit(solution)/shard_map/all_gather | solution.py:145
  124.1 177.6 %all-gather.10.cloned.1.call-start = ((), (), s32[]{:S(2)}) async-start(), calls=%async_computation.10 | async-start | bytes 4866048 | tf_op jit(solution)/shard_map/all_gather | solution.py:147
  265.9 9.0 copy-start.68
  270.9 19.5 %all-to-all-start.1 = ((bf16[2,1024,384]{2,0,1:T(2,128)(2,1)}), bf16[2,1024,384]{2,0,1:T(2,128)(2,1)S(1)}, u32[]{:S(2)}, u32[]{:S(2)}) async-start(bf16[2,1024,384]{2,0,1:T(2,128)(2,1)} %copy.108), calls=%async_computation.1 | async-start | bytes 3145728 | tf_op jit(solution)/shard_map/all_to_all | solution.py:179
  274.6 180.8 %reduce-scatter.12.cloned.1.call-start = ((), (), s32[]{:S(2)}) async-start(), calls=%async_computation.14 | async-start | bytes 9732096 | tf_op jit(solution)/shard_map/reduce_scatter | solution.py:249
  276.6 33.4 %copy-start.15 = (bf16[2,512,768]{2,1,0:T(8,128)(2,1)}, bf16[2,512,768]{2,1,0:T(8,128)(2,1)S(1)}, u32[]{:S(2)}) copy-start(bf16[2,512,768]{2,1,0:T(8,128)(2,1)S(1)} %broadcast_select_fusion) | copy-start | bytes 4718596
  299.5 249.0 %copy-start.37 = (f32[1024]{0:T(1024)}, f32[1024]{0:T(1024)S(1)}, u32[]{:S(2)}) copy-start(f32[1024]{0:T(1024)S(1)} %broadcast_multiply_fusion) | copy-start | bytes 12292
  301.7 246.9 %copy-start.44 = (f32[1024]{0:T(1024)}, f32[1024]{0:T(1024)S(1)}, u32[]{:S(2)}) copy-start(f32[1024]{0:T(1024)S(1)} %fusion.57) | copy-start | bytes 12292
  323.6 131.9 %copy-start.39 = (f32[96,768]{1,0:T(8,128)S(1)}, f32[96,768]{1,0:T(8,128)}, u32[]{:S(2)}) copy-start(f32[96,768]{1,0:T(8,128)} %param.42) | copy-start | bytes 884740
  323.6 131.9 %copy-start.40 = (f32[96,768]{1,0:T(8,128)S(1)}, f32[96,768]{1,0:T(8,128)}, u32[]{:S(2)}) copy-start(f32[96,768]{1,0:T(8,128)} %param.40) | copy-start | bytes 884740
  323.6 131.9 %copy-start.41 = (f32[96,768]{1,0:T(8,128)S(1)}, f32[96,768]{1,0:T(8,128)}, u32[]{:S(2)}) copy-start(f32[96,768]{1,0:T(8,128)} %param.41) | copy-start | bytes 884740
  323.6 198.3 %all-gather.12.cloned.1.call-start = ((), (), s32[]{:S(2)}) async-start(), calls=%async_computation.11 | async-start | bytes 4866048 | tf_op jit(solution)/shard_map/all_gather | solution.py:148
  457.5 80.2 %copy-start.8 = (f32[1024,768]{1,0:T(8,128)S(1)}, f32[1024,768]{1,0:T(8,128)}, u32[]{:S(2)}) copy-start(f32[1024,768]{1,0:T(8,128)} %copy-done.7) | copy-start | bytes 9437188
  537.7 10.9 copy-start.19
  556.7 23.6 %all-to-all-start.2 = ((bf16[2,512,768]{1,0,2:T(2,128)(2,1)}), bf16[2,512,768]{1,0,2:T(2,128)(2,1)S(1)}, u32[]{:S(2)}, u32[]{:S(2)}) async-start(bf16[2,512,768]{1,0,2:T(2,128)(2,1)} %copy.110), calls=%async_computation.2 | async-start | bytes 3145728 | tf_op jit(solution)/shard_map/all_to_all | solution.py:215
  598.8 7.2 copy-start.6
  606.0 6.9 copy-start.11
  623.4 7.2 copy-start.6
  630.6 6.9 copy-start.11
  664.6 7.2 copy-start.6
  671.8 6.9 copy-start.11
  689.2 7.2 copy-start.6
  734.3 59.0 %all-to-all-start.3 = ((bf16[3,2,1024,384]{3,1,0,2:T(2,128)(2,1)}), bf16[3,2,1024,384]{3,1,0,2:T(2,128)(2,1)}, u32[]{:S(2)}, u32[]{:S(2)}) async-start(bf16[3,2,1024,384]{3,1,0,2:T(2,128)(2,1)} %copy.116), calls=%async_computation.3 | async-start | bytes 9437184 | tf_op jit(solution)/shard_map/all_to_all | solution.py:235
  740.3 150.5 %reduce-scatter.8.cloned.1.call-start = ((), (), s32[]{:S(2)}) async-start(), calls=%async_computation.12 | async-start | bytes 2433024 | tf_op jit(solution)/shard_map/reduce_scatter | solution.py:247
  743.3 220.4 %reduce-scatter.14.cloned.1.call-start = ((), (), s32[]{:S(2)}) async-start(), calls=%async_computation.15 | async-start | bytes 6082560
  816.5 287.8 %reduce-scatter.10.cloned.1.call-start = ((), (), s32[]{:S(2)}) async-start(), calls=%async_computation.13 | async-start | bytes 9732096 | tf_op jit(solution)/shard_map/reduce_scatter | solution.py:248
  829.8 13.3 %copy-start.4 = (bf16[2,512,768]{2,1,0:T(8,128)(2,1)S(1)}, bf16[2,512,768]{2,1,0:T(8,128)(2,1)}, u32[]{:S(2)}) copy-start(bf16[2,512,768]{2,1,0:T(8,128)(2,1)} %param.27) | copy-start | bytes 4718596
  829.8 13.3 %copy-start.25 = (bf16[128,8,2,384]{3,1,2,0:T(8,128)(2,1)S(1)}, bf16[128,8,2,384]{3,1,2,0:T(8,128)(2,1)}, u32[]{:S(2)}) copy-start(bf16[128,8,2,384]{3,1,2,0:T(8,128)(2,1)} %copy-done.24) | copy-start | bytes 4718596
  829.8 13.3 %copy-start.27 = (bf16[128,8,2,384]{3,1,2,0:T(8,128)(2,1)S(1)}, bf16[128,8,2,384]{3,1,2,0:T(8,128)(2,1)}, u32[]{:S(2)}) copy-start(bf16[128,8,2,384]{3,1,2,0:T(8,128)(2,1)} %copy-done.26) | copy-start | bytes 4718596
  829.8 13.3 %copy-start.34 = (bf16[1024,384]{1,0:T(8,128)(2,1)S(1)}, bf16[1024,384]{1,0:T(8,128)(2,1)}, u32[]{:S(2)}) copy-start(bf16[1024,384]{1,0:T(8,128)(2,1)} %copy-done.33) | copy-start | bytes 2359300
  829.8 13.3 %copy-start.53 = (f32[768]{0:T(1024)S(1)}, f32[768]{0:T(1024)}, u32[]{:S(2)}) copy-start(f32[768]{0:T(1024)} %copy-done.52) | copy-start | bytes 9220
  829.9 13.2 %copy-start.55 = (f32[1,4,2,128]{3,1,2,0:T(4,128)S(1)}, f32[1,4,2,128]{3,1,2,0:T(4,128)}, u32[]{:S(2)}) copy-start(f32[1,4,2,128]{3,1,2,0:T(4,128)} %copy-done.54) | copy-start | bytes 12292
  829.9 13.2 %copy-start.69 = (bf16[768,1920]{1,0:T(8,128)(2,1)S(1)}, bf16[768,1920]{1,0:T(8,128)(2,1)}, u32[]{:S(2)}) copy-start(bf16[768,1920]{1,0:T(8,128)(2,1)} %all-gather.6.cloned.1.call-done) | copy-start | bytes 8847364
  846.8 43.4 %copy-start.63 = (f32[24,4]{0,1:T(4,128)S(1)}, f32[24,4]{0,1:T(4,128)}, u32[]{:S(2)}) copy-start(f32[24,4]{0,1:T(4,128)} %param.43) | copy-start | bytes 1156
  846.8 43.4 %copy-start.66 = (f32[24,4]{0,1:T(4,128)S(1)}, f32[24,4]{0,1:T(4,128)}, u32[]{:S(2)}) copy-start(f32[24,4]{0,1:T(4,128)} %param.45) | copy-start | bytes 1156
  846.8 43.4 %copy-start.67 = (f32[24,4]{0,1:T(4,128)S(1)}, f32[24,4]{0,1:T(4,128)}, u32[]{:S(2)}) copy-start(f32[24,4]{0,1:T(4,128)} %param.44) | copy-start | bytes 1156
  846.9 44.0 %copy-start.43 = (f32[24,768]{1,0:T(8,128)S(1)}, f32[24,768]{1,0:T(8,128)}, u32[]{:S(2)}) copy-start(f32[24,768]{1,0:T(8,128)} %param.34) | copy-start | bytes 221188
  846.9 44.0 %copy-start.48 = (f32[24,768]{1,0:T(8,128)S(1)}, f32[24,768]{1,0:T(8,128)}, u32[]{:S(2)}) copy-start(f32[24,768]{1,0:T(8,128)} %param.36) | copy-start | bytes 221188
  846.9 44.0 %copy-start.49 = (f32[24,768]{1,0:T(8,128)S(1)}, f32[24,768]{1,0:T(8,128)}, u32[]{:S(2)}) copy-start(f32[24,768]{1,0:T(8,128)} %param.35) | copy-start | bytes 221188
  846.9 45.6 %copy-start.17 = (bf16[2,512,768]{2,1,0:T(8,128)(2,1)S(1)}, bf16[2,512,768]{2,1,0:T(8,128)(2,1)}, u32[]{:S(2)}) copy-start(bf16[2,512,768]{2,1,0:T(8,128)(2,1)} %copy-done.15) | copy-start | bytes 4718596
  846.9 45.6 %copy-start.61 = (f32[1024]{0:T(1024)S(1)}, f32[1024]{0:T(1024)}, u32[]{:S(2)}) copy-start(f32[1024]{0:T(1024)} %copy-done.60) | copy-start | bytes 12292
  892.5 211.8 %copy-start.31 = (f32[24,3072]{1,0:T(8,128)S(1)}, f32[24,3072]{1,0:T(8,128)}, u32[]{:S(2)}) copy-start(f32[24,3072]{1,0:T(8,128)} %param.37) | copy-start | bytes 884740
  (60 other events, 168.7 us)
Sparse Core Ops, SparseCore 0:
  11.5 61.5 all-gather.5
  127.7 52.4 all-gather.7
  183.6 62.6 all-gather.9
  323.8 131.6 reduce-scatter.11
  459.2 62.6 all-gather.11
  747.0 99.2 reduce-scatter.7
  851.9 111.6 reduce-scatter.13
  969.6 134.6 reduce-scatter.9
where the time goes:
time: 1120 us; the launch traced here: 1110 us
  waiting for transfers between devices  537 us (48%)
  matrix products  182 us (16%)
  local copies, waits for them, and re-layouts  153 us (14%)
  blocking collectives  110 us (10%)
  other arithmetic  95.3 us (9%)
  starting transfers between devices  20 us (2%)
  between operations  15.3 us (1%)
    reduce_scatter x1, waiting for transfers between devices, body(): lax.psum_scatter(grad_up, ('dp', 'seq'), scatter_dimension=0, tiled=True)  139 us
    reduce_scatter x1, waiting for transfers between devices, body(): lax.psum_scatter(grad_down, ('dp', 'seq'), scatter_dimension=0, tiled=True)  132 us
    all_gather x1, blocking collectives, body(): lax.all_gather(norm_master.astype(jnp.bfloat16), ('dp', 'seq'), axis=0, t...  69.8 us
    unnamed x9, waiting for transfers between devices  66.8 us
    all_gather x1, waiting for transfers between devices, body(): lax.all_gather(down_master.astype(jnp.bfloat16), ('dp', 'seq'), axis=0, t...  64.4 us
    all_to_all x1, waiting for transfers between devices, body(): lax.all_to_all(stacked, 'seq', split_axis=3, concat_axis=2, tiled=True)  51.9 us
    all_to_all x1, waiting for transfers between devices, body(): lax.all_to_all(stacked_grads, 'seq', split_axis=2, concat_axis=3, tiled=T...  49.9 us
    unnamed x1, blocking collectives  39.8 us
  transfers between devices with their start and end apart: 12, of which 8 were waited for; matrix products, arithmetic and copies ran while one was open for 16% of the time, Pallas kernels for 0%

commit v1 on v0

v1 whole, which is shorter than its diff:
```python
import functools

import jax
import jax.numpy as jnp
from jax import lax
from jax.experimental import pallas as pl
from jax.experimental.pallas import tpu as pltpu
from jax.sharding import PartitionSpec as P

HEAD_DIM = 64
LANES = 128
EPSILON = 1e-05
MOMENTUM = 0.5
AVERAGING = 0.5
RATE = 0.0006
SCALE = HEAD_DIM ** (-0.5)
VMEM_BYTES = 48 << 20

BF16 = jnp.bfloat16
F32 = jnp.float32


def times_transposed(left, right):
    return lax.dot_general(left, right, (((1,), (1,)), ((), ())), preferred_element_type=F32)


def times(left, right):
    return lax.dot_general(left, right, (((1,), (0,)), ((), ())), preferred_element_type=F32)


def contract_rows(left, right):
    return lax.dot_general(left, right, (((0,), (0,)), ((), ())), preferred_element_type=F32)


def attend_forward_kernel(
    tile, fresh_pairs, q_ref, k_ref, fresh_ref, reused_ref, out_ref, totals_ref
):
    length = q_ref.shape[0]
    first = lax.broadcasted_iota(jnp.int32, (1, LANES), 1) < HEAD_DIM
    values = jnp.where(pl.program_id(1) < fresh_pairs, fresh_ref[...], reused_ref[...])
    row = lax.broadcasted_iota(jnp.int32, (tile, tile), 0)
    column = lax.broadcasted_iota(jnp.int32, (tile, tile), 1)
    for block in range(length // tile):
        start, stop = block * tile, (block + 1) * tile
        queries = q_ref[start:stop, :] * jnp.asarray(SCALE, BF16)
        outputs, totals = [], []
        for own in (first, ~first):
            scores = times_transposed(
                jnp.where(own, queries, jnp.zeros((), BF16)), k_ref[:stop, :]
            )
            diagonal = jnp.where(row >= column, scores[:, start:], -1e30)
            scores = (
                diagonal if block == 0 else jnp.concatenate([scores[:, :start], diagonal], 1)
            )
            maximum = jnp.max(scores, 1, keepdims=True)
            weights = jnp.exp(scores - maximum)
            summed = jnp.sum(weights, 1, keepdims=True)
            outputs.append(times(weights.astype(BF16), values[:stop, :]) * (1.0 / summed))
            totals.append(maximum + jnp.log(summed))
        out_ref[start:stop, :] = jnp.where(first, outputs[0], outputs[1]).astype(BF16)
        turned = jnp.where(first, totals[0], totals[1]).T
        totals_ref[0:1, start:stop] = turned[0:1, :]
        totals_ref[1:2, start:stop] = turned[HEAD_DIM : HEAD_DIM + 1, :]


def attend_backward_kernel(
    tile,
    fresh_pairs,
    q_ref,
    k_ref,
    fresh_ref,
    reused_ref,
    out_ref,
    grad_ref,
    totals_ref,
    grad_q_ref,
    grad_k_ref,
    grad_v_ref,
    sum_q_ref,
):
    length = q_ref.shape[0]
    first = lax.broadcasted_iota(jnp.int32, (1, LANES), 1) < HEAD_DIM
    values = jnp.where(pl.program_id(1) < fresh_pairs, fresh_ref[...], reused_ref[...])
    head_of_lane = lax.broadcasted_iota(jnp.int32, (8, LANES), 1) // HEAD_DIM
    pick = jnp.where(
        head_of_lane == lax.broadcasted_iota(jnp.int32, (8, LANES), 0), 1.0, 0.0
    ).astype(BF16)
    product = out_ref[...].astype(F32) * grad_ref[...].astype(F32)
    coarse = product.astype(BF16)
    fine = (product - coarse.astype(F32)).astype(BF16)
    inner = times_transposed(pick, coarse) + times_transposed(pick, fine)
    row = lax.broadcasted_iota(jnp.int32, (tile, tile), 0)
    column = lax.broadcasted_iota(jnp.int32, (tile, tile), 1)
    for start in range(0, length, tile):
        stop = start + tile
        keys = k_ref[start:stop, :] * jnp.asarray(SCALE, BF16)
        own_values = values[start:stop, :]
        queries, grads = q_ref[start:, :], grad_ref[start:, :]
        grad_keys, grad_values = [], []
        for head, own in enumerate((first, ~first)):
            own_keys = jnp.where(own, keys, jnp.zeros((), BF16))
            scores = times_transposed(own_keys, queries)
            probs = jnp.exp(scores - totals_ref[head : head + 1, start:])
            diagonal = jnp.where(column >= row, probs[:, :tile], 0.0)
            probs = (
                diagonal if stop == length else jnp.concatenate([diagonal, probs[:, tile:]], 1)
            )
            grad_probs = times_transposed(
                jnp.where(own, own_values, jnp.zeros((), BF16)), grads
            )
            grad_scores = (probs * (grad_probs - inner[head : head + 1, start:])).astype(BF16)
            grad_values.append(times(probs.astype(BF16), grads))
            grad_keys.append(times(grad_scores, queries))
            part = contract_rows(grad_scores, own_keys)
            if start == 0 and head == 0:
                sum_q_ref[...] = part
            else:
                sum_q_ref[start:, :] += part
        grad_k_ref[start:stop, :] = (
            jnp.where(first, grad_keys[0], grad_keys[1]) * SCALE
        ).astype(BF16)
        grad_v_ref[start:stop, :] = jnp.where(first, grad_values[0], grad_values[1]).astype(BF16)
    grad_q_ref[...] = sum_q_ref[...].astype(BF16)


def head_specs(length, pairs):
    fresh_pairs = pairs // 2
    return [
        pl.BlockSpec((length, LANES), lambda s, p: (s, p)),
        pl.BlockSpec((length, LANES), lambda s, p: (s, pairs + p)),
        pl.BlockSpec(
            (length, LANES), lambda s, p: (s, 2 * pairs + jnp.minimum(p, fresh_pairs - 1))
        ),
        pl.BlockSpec((length, LANES), lambda s, p: (s, jnp.maximum(p - fresh_pairs, 0))),
    ]


def attend_forward(projected, reused, length, width):
    count, pairs = projected.shape[0] // length, width // LANES
    area = count * length * length * width
    return pl.pallas_call(
        functools.partial(attend_forward_kernel, min(512, length), pairs // 2),
        grid=(count, pairs),
        in_specs=head_specs(length, pairs),
        out_specs=[
            pl.BlockSpec((length, LANES), lambda s, p: (s, p)),
            pl.BlockSpec((None, None, 2, length), lambda s, p: (s, p, 0, 0)),
        ],
        out_shape=[
            jax.ShapeDtypeStruct((count * length, width), BF16),
            jax.ShapeDtypeStruct((count, pairs, 2, length), F32),
        ],
        compiler_params=pltpu.CompilerParams(vmem_limit_bytes=VMEM_BYTES),
        cost_estimate=pl.CostEstimate(
            flops=12 * area,
            bytes_accessed=8 * count * length * width,
            transcendentals=area // HEAD_DIM,
        ),
        name="attend_forward",
    )(projected, projected, projected, reused)


def attend_backward(projected, reused, attended, grads, totals, length, width):
    count, pairs = projected.shape[0] // length, width // LANES
    area = count * length * length * width
    columns = pl.BlockSpec((length, LANES), lambda s, p: (s, p))
    return pl.pallas_call(
        functools.partial(attend_backward_kernel, min(256, length), pairs // 2),
        grid=(count, pairs),
        in_specs=head_specs(length, pairs)
        + [
            columns,
            columns,
            pl.BlockSpec((None, None, 2, length), lambda s, p: (s, p, 0, 0)),
        ],
        out_specs=[columns] * 3,
        out_shape=[jax.ShapeDtypeStruct((count * length, width), BF16)] * 3,
        scratch_shapes=[pltpu.VMEM((length, LANES), F32)],
        compiler_params=pltpu.CompilerParams(vmem_limit_bytes=VMEM_BYTES),
        cost_estimate=pl.CostEstimate(
            flops=24 * area,
            bytes_accessed=16 * count * length * width,
            transcendentals=area // HEAD_DIM,
        ),
        name="attend_backward",
    )(projected, projected, projected, reused, attended, grads, totals)


class Grid:
    def __init__(self, mesh):
        dp, self.halves = mesh.shape["dp"], mesh.shape["seq"]
        assert self.halves == 2 and dp & (dp - 1) == 0
        self.dp = dp
        self.dp_bits = dp.bit_length() - 1
        self.bits = self.dp_bits + 1
        core, near = self.dp_bits - 1, self.dp_bits - 2
        seq = self.dp_bits
        far = list(range(self.dp_bits - 2))
        self.orders = (far + [near, seq, core], far + [seq, near, core])

    def bit(self, which):
        if which == self.dp_bits:
            return lax.axis_index("seq")
        return (lax.axis_index("dp") >> (self.dp_bits - 1 - which)) & 1

    def swap(self, array, which):
        if which == self.dp_bits:
            return lax.ppermute(array, "seq", [(0, 1), (1, 0)])
        mask = 1 << (self.dp_bits - 1 - which)
        return lax.ppermute(array, "dp", [(i, i ^ mask) for i in range(self.dp)])

    def gather(self, shard, order):
        done, whole = [], shard
        for which in order:
            other = self.swap(whole, which)
            place = sum(1 for d in done if d < which)
            low = self.bit(which) == 0
            whole = jnp.stack(
                [jnp.where(low, whole, other), jnp.where(low, other, whole)], place
            )
            done.append(which)
        return whole.reshape(-1, shard.shape[-1])

    def scatter_sum(self, partial, order):
        rows, columns = partial.shape
        whole = partial.reshape((2,) * self.bits + (rows >> self.bits, columns))
        left = list(range(self.bits))
        for which in reversed(order):
            place = left.index(which)
            bit = self.bit(which)
            away = lax.dynamic_index_in_dim(whole, 1 - bit, place, keepdims=False)
            keep = lax.dynamic_index_in_dim(whole, bit, place, keepdims=False)
            left.remove(which)
            whole = keep.astype(F32) + self.swap(away, which).astype(F32)
            if left:
                whole = whole.astype(BF16)
        return whole

    def to_whole(self, array):
        count, half, width = array.shape
        seq = lax.axis_index("seq")
        split = array.reshape(2, count // 2, half, width)
        keep = lax.dynamic_index_in_dim(split, seq, 0, keepdims=False)
        other = self.swap(
            lax.dynamic_index_in_dim(split, 1 - seq, 0, keepdims=False), self.dp_bits
        )
        low = seq == 0
        return jnp.stack(
            [jnp.where(low, keep, other), jnp.where(low, other, keep)], 1
        ).reshape(count * half, width)

    def to_halves(self, array, half):
        width = array.shape[-1]
        seq = lax.axis_index("seq")
        split = array.reshape(-1, 2, half, width)
        keep = lax.dynamic_index_in_dim(split, seq, 1, keepdims=False)
        other = self.swap(
            lax.dynamic_index_in_dim(split, 1 - seq, 1, keepdims=False), self.dp_bits
        )
        low = seq == 0
        return jnp.concatenate([jnp.where(low, keep, other), jnp.where(low, other, keep)], 0)


def normalize(values):
    center = values - jnp.mean(values, -1, keepdims=True)
    spread = jnp.mean(center * center, -1, keepdims=True)
    inverse = lax.rsqrt(spread + EPSILON)
    return center * inverse, inverse


def normalize_back(grad, unit, inverse, gain):
    scaled = grad * gain
    along = jnp.mean(scaled * unit, -1, keepdims=True)
    level = jnp.mean(scaled, -1, keepdims=True)
    return inverse * (scaled - level - unit * along)


def gelu_tanh(values):
    return jax.nn.gelu(values, approximate=True)


def update(gradient, moment, master, average):
    moment_new = MOMENTUM * moment + gradient
    master_new = master - RATE * (gradient + MOMENTUM * moment_new)
    average_new = AVERAGING * average + (1.0 - AVERAGING) * master_new
    return (moment_new, master_new, average_new)


def body(
    grid,
    tokens,
    first_values,
    cotangent,
    lengths,
    qkv_master,
    qkv_moment,
    qkv_average,
    out_master,
    out_moment,
    out_average,
    up_master,
    up_moment,
    up_average,
    down_master,
    down_moment,
    down_average,
    norm_master,
    norm_moment,
    norm_average,
):
    count, half, width = tokens.shape
    length = 2 * half
    order_x, order_y = grid.orders
    norm_columns = norm_master.shape[1]
    qkv_columns = qkv_master.shape[1]

    rows_in = grid.to_whole(tokens).astype(F32)
    norm_padded = jnp.pad(norm_master, ((0, 0), (0, LANES - norm_columns)))
    work = jnp.concatenate([norm_padded, qkv_master], 1).astype(BF16)
    cut = (work.shape[1] // 2) // LANES * LANES
    work = jnp.concatenate(
        [grid.gather(work[:, :cut], order_x), grid.gather(work[:, cut:], order_y)], 1
    )
    norm_param = work[:, :norm_columns].astype(F32)
    w_qkv = work[:, LANES:]
    gain_one, shift_one = norm_param[:, 0], norm_param[:, 1]
    gain_two, shift_two = norm_param[:, 2], norm_param[:, 3]
    reused = grid.to_whole(first_values)
    w_out = grid.gather(out_master.astype(BF16), order_x)
    w_up = grid.gather(up_master.astype(BF16), order_x)
    w_down = grid.gather(down_master.astype(BF16), order_y)
    whole_cotangent = grid.to_whole(cotangent)

    unit_one, inverse_one = normalize(rows_in)
    normed_one = (unit_one * gain_one + shift_one).astype(BF16)
    projected = times(normed_one, w_qkv).astype(BF16)
    attended, totals = attend_forward(projected, reused, length, width)
    mid_rows = rows_in + times(attended, w_out)
    unit_two, inverse_two = normalize(mid_rows)
    normed_two = (unit_two * gain_two + shift_two).astype(BF16)
    hidden_pre = times(normed_two, w_up)
    hidden, pull_gelu = jax.vjp(gelu_tanh, hidden_pre)
    hidden = hidden.astype(BF16)
    mixed = grid.to_halves((mid_rows + times(hidden, w_down)).astype(BF16), half)

    own_lengths = lax.dynamic_index_in_dim(
        lengths.reshape(2, count // 2), lax.axis_index("seq"), 0, keepdims=False
    )
    position = lax.iota(jnp.int32, length)
    keep_mask = (position[None, :] < own_lengths[:, None]).reshape(-1)
    grad_mixed = jnp.where(keep_mask[:, None], whole_cotangent, jnp.zeros((), BF16))
    grad_down = contract_rows(hidden, grad_mixed).astype(BF16)
    sum_down = grid.scatter_sum(grad_down, order_y)
    grad_hidden = pull_gelu(times_transposed(grad_mixed, w_down))[0].astype(BF16)
    grad_up = contract_rows(normed_two, grad_hidden).astype(BF16)
    sum_up = grid.scatter_sum(grad_up, order_x)
    grad_normed_two = times_transposed(grad_hidden, w_up)
    grad_gain_two = jnp.sum(grad_normed_two * unit_two, 0)
    grad_shift_two = jnp.sum(grad_normed_two, 0)
    grad_mid = grad_mixed.astype(F32) + normalize_back(
        grad_normed_two, unit_two, inverse_two, gain_two
    )
    grad_mid_low = grad_mid.astype(BF16)
    grad_out = contract_rows(attended, grad_mid_low).astype(BF16)
    sum_out = grid.scatter_sum(grad_out, order_x)
    grad_attended = times_transposed(grad_mid_low, w_out).astype(BF16)
    grad_q, grad_k, grad_v = attend_backward(
        projected, reused, attended, grad_attended, totals, length, width
    )
    first_grad = grid.to_halves(grad_v[:, width // 2 :], half)
    grad_columns = jnp.concatenate([grad_q, grad_k, grad_v[:, : width // 2]], 1)
    grad_normed_one = times_transposed(grad_columns, w_qkv)
    tokens_grad = grid.to_halves(
        (grad_mid + normalize_back(grad_normed_one, unit_one, inverse_one, gain_one)).astype(
            BF16
        ),
        half,
    )
    grad_norm = jnp.stack(
        [
            jnp.sum(grad_normed_one * unit_one, 0),
            jnp.sum(grad_normed_one, 0),
            grad_gain_two,
            grad_shift_two,
        ],
        1,
    )
    grad_work = jnp.concatenate(
        [
            jnp.pad(grad_norm, ((0, 0), (0, LANES - norm_columns))),
            contract_rows(normed_one, grad_columns),
        ],
        1,
    ).astype(BF16)
    sum_work = jnp.concatenate(
        [
            grid.scatter_sum(grad_work[:, :cut], order_x),
            grid.scatter_sum(grad_work[:, cut:], order_y),
        ],
        1,
    )
    sum_norm, sum_qkv = sum_work[:, :norm_columns], sum_work[:, LANES:]
    return (
        mixed,
        tokens_grad,
        first_grad,
        *update(sum_qkv, qkv_moment, qkv_master, qkv_average),
        *update(sum_out, out_moment, out_master, out_average),
        *update(sum_up, up_moment, up_master, up_average),
        *update(sum_down, down_moment, down_master, down_average),
        *update(sum_norm, norm_moment, norm_master, norm_average),
    )


def solution(mesh):
    activation = P("dp", "seq", None)
    parameter = P(("dp", "seq"), None)
    return jax.shard_map(
        functools.partial(body, Grid(mesh)),
        mesh=mesh,
        in_specs=(activation,) * 3 + (P("dp"),) + (parameter,) * 15,
        out_specs=(activation,) * 3 + (parameter,) * 15,
        check_vma=False,
    )
```

time: 1120 us -> 455 us (0.41)
  waiting for transfers between devices: 537 us -> 134 us
  blocking collectives: 110 us -> 0 us
  local copies, waits for them, and re-layouts: 153 us -> 50.9 us
  matrix products: 182 us -> 88.7 us
  Pallas kernels: 0 us -> 45.2 us
  starting transfers between devices: 20 us -> 60.6 us
  other arithmetic: 95.3 us -> 65.5 us
  between operations: 15.3 us -> 2.53 us
    reduce_scatter x3 -> x0, waiting for transfers between devices: 270 us -> none  [the longest x1 139 us: body(): lax.psum_scatter(grad_up, ('dp', 'seq'), scatter_dimension=0, tiled=True)]
    all_to_all x4 -> x0, waiting for transfers between devices: 136 us -> none  [the longest x1 51.9 us: body(): lax.all_to_all(stacked, 'seq', split_axis=3, concat_axis=2, tiled=True)]
    ppermute x0 -> x56, waiting for transfers between devices: none -> 134 us  [the longest x40 85.7 us: swap(): return lax.ppermute(array, 'dp', [(i, i ^ mask) for i in range(self.dp)])]
    dot_general x32 -> x4, matrix products: 122 us -> 31.4 us  [times(): lax.dot_general(left, right, (((1,), (0,)), ((), ())), preferred_element_...]
    all_gather x1 -> x0, blocking collectives: 69.8 us -> none  [body(): lax.all_gather(norm_master.astype(jnp.bfloat16), ('dp', 'seq'), axis=0, t...]
    unnamed x9 -> x0, waiting for transfers between devices: 66.8 us -> none
    all_gather x4 -> x0, waiting for transfers between devices: 64.4 us -> none  [the longest x1 64.4 us: body(): lax.all_gather(down_master.astype(jnp.bfloat16), ('dp', 'seq'), axis=0, t...]
    ppermute x0 -> x56, starting transfers between devices: none -> 60.6 us  [the longest x40 42.4 us: swap(): return lax.ppermute(array, 'dp', [(i, i ^ mask) for i in range(self.dp)])]
  transfers between devices with their start and end apart: 12 -> 56, of which waited for: 8 -> 28; matrix products, arithmetic and copies ran while one was open for 16% -> 26% of each run, Pallas kernels for 0% -> 4%
where the time goes in v1:
time: 455 us; the launch traced here: 447 us
  waiting for transfers between devices  134 us (29%)
  matrix products  88.7 us (19%)
  other arithmetic  65.5 us (14%)
  starting transfers between devices  60.6 us (13%)
  local copies, waits for them, and re-layouts  50.9 us (11%)
  Pallas kernels  45.2 us (10%)
    ppermute x40, waiting for transfers between devices, swap(): return lax.ppermute(array, 'dp', [(i, i ^ mask) for i in range(self.dp)])  85.7 us
    ppermute x16, waiting for transfers between devices, swap(): return lax.ppermute(array, 'seq', [(0, 1), (1, 0)])  48.5 us
    ppermute x40, starting transfers between devices, swap(): return lax.ppermute(array, 'dp', [(i, i ^ mask) for i in range(self.dp)])  42.4 us
    dot_general x4, matrix products, times(): lax.dot_general(left, right, (((1,), (0,)), ((), ())), preferred_element_...  31.4 us
    dot_general x4, matrix products, times_transposed(): lax.dot_general(left, right, (((1,), (1,)), ((), ())), preferred_element_...  29.6 us
    dot_general x4, matrix products, contract_rows(): lax.dot_general(left, right, (((0,), (0,)), ((), ())), preferred_element_...  27.6 us
    pallas_call x1, Pallas kernels, attend_backward(): pl.pallas_call(functools.partial(attend_backward_kernel, min(256, length)...  27 us
    convert_element_type x20, other arithmetic, scatter_sum(): whole = whole.astype(BF16)  21.8 us
  transfers between devices with their start and end apart: 56, of which 28 were waited for; matrix products, arithmetic and copies ran while one was open for 26% of the time, Pallas kernels for 4%

profile of v1, /device:TPU:0, one launch (start us, length us, event | category | flops | bytes accessed | tf_op | source)
XLA Modules:
  0.0 447.5 jit_solution(5078319710139230680)
XLA Ops:
  2.4 4.0 collective-permute-start.6
  12.3 2.9 collective-permute-start.22
  22.8 3.0 collective-permute-start.1
  25.8 5.9 %collective-permute-done.1 = bf16[24,1024]{1,0:T(8,128)(2,1)S(1)} collective-permute-done((bf16[24,1024]{1,0:T(8,128)(2,1)S(1)}, bf16[24,1024]{1,0:T(8,128)(2,1)S(1)}, u32[]{:S(2)}, u32[]{:S(2)}) %collective-permute-start.1) | collective-permute-done | bytes 49184 | tf_op jit(solution)/shard_map/ppermute | solution.py:210
  31.8 4.3 collective-permute-done.13
  44.5 3.0 collective-permute-done.14
  47.6 10.5 %collective-permute-done.8 = bf16[2,2,24,1024]{3,2,1,0:T(8,128)(2,1)S(1)} collective-permute-done((bf16[2,2,24,1024]{3,2,1,0:T(8,128)(2,1)S(1)}, bf16[2,2,24,1024]{3,2,1,0:T(8,128)(2,1)S(1)}, u32[]{:S(2)}, u32[]{:S(2)}) %collective-permute-start.8) | collective-permute-done | bytes 196640 | tf_op jit(solution)/shard_map/ppermute | solution.py:208
  60.1 4.1 collective-permute-done.3
  68.5 5.9 %collective-permute-done.15 = bf16[2,2,2,24,768]{4,3,2,1,0:T(8,128)(2,1)S(1)} collective-permute-done((bf16[2,2,2,24,768]{4,3,2,1,0:T(8,128)(2,1)S(1)}, bf16[2,2,2,24,768]{4,3,2,1,0:T(8,128)(2,1)S(1)}, u32[]{:S(2)}, u32[]{:S(2)}) %collective-permute-start.15) | collective-permute-done | bytes 294944 | tf_op jit(solution)/shard_map/ppermute | solution.py:208
  79.4 3.4 collective-permute-done.4
  97.5 5.1 %convolution_convert_fusion.2.q_ref.k_ref.fresh_ref = bf16[1024,1920]{1,0:T(8,128)(2,1)} fusion(bf16[1024,768]{1,0:T(8,128)(2,1)S(1)} %fusion.19, bf16[768,1024]{1,0:T(8,128)(2,1)S(1)} %bitcast.392, bf16[768,1024]{1,0:T(8,128)(2,1)S(1)} %bitcast.390), kind=kOutput, calls=%fused_computation.23 | convolution fusion | flops 3027763200 | bytes 8650752 | tf_op jit(solution)/shard_map/dot_general | solution.py:28
  102.7 14.7 %collective-permute-done.25 = bf16[2,2,2,96,768]{4,3,2,1,0:T(8,128)(2,1)S(1)} collective-permute-done((bf16[2,2,2,96,768]{4,3,2,1,0:T(8,128)(2,1)S(1)}, bf16[2,2,2,96,768]{4,3,2,1,0:T(8,128)(2,1)S(1)}, u32[]{:S(2)}, u32[]{:S(2)}) %collective-permute-start.25) | collective-permute-done | bytes 1179680 | tf_op jit(solution)/shard_map/ppermute | solution.py:210
  120.9 18.1 %attend_forward.1 = (bf16[1024,768]{1,0:T(8,128)(2,1)S(1)}, f32[1,6,2,1024]{3,2,1,0:T(2,128)S(1)}) custom-call(bf16[1024,1920]{1,0:T(8,128)(2,1)} %convolution_convert_fusion.2.q_ref.k_ref.fresh_ref, bf16[1024,1920]{1,0:T(8,128)(2,1)} %convolution_convert_fusion.2.q_ref.k_ref.fresh_ref, bf16[1024,1920]{1,0:T(8,128)(2,1)} %convolution_convert_fusion.2.q_ref.k_ref.fresh_ref, ...), custom_call_target="tpu_custom_call" | custom-call | flops 9663676416 | bytes 6291456 | tf_op jit(solution)/shard_map/attend_forward/pallas_call | solution.py:141
  139.1 3.9 fusion.55
  145.9 3.7 select_bitcast_fusion.3
  149.6 2.6 pad_maximum_fusion
  152.3 10.6 %fusion.53 = f32[1024,3072]{1,0:T(8,128)} fusion(bf16[768,3072]{1,0:T(8,128)(2,1)} %bitcast.382, f32[1024,768]{1,0:T(8,128)S(1)} %get-tuple-element.191, f32[768]{0:T(1024)S(1)} %get-tuple-element.91, f32[768]{0:T(1024)S(1)} %get-tuple-element.90, f32[1024]{0:T(1024)S(1)} %add_rsqrt_fusion, f32[1024]{0:T(1024)S(1)} %broadcast_multiply_fusion.4), kind=kOutput, calls=%fused_computation.272 | convolution fusion | flops 4835770368 | bytes 20461568 | tf_op jit(solution)/shard_map/dot_general | solution.py:28
  162.9 11.8 %add_convert_fusion = bf16[1024,768]{1,0:T(8,128)(2,1)} fusion(f32[1024,768]{1,0:T(8,128)S(1)} %get-tuple-element.191, bf16[3072,768]{1,0:T(8,128)(2,1)S(1)} %bitcast.380, f32[1024,3072]{1,0:T(8,128)} %fusion.53), kind=kOutput, calls=%fused_computation.48 | convolution fusion | flops 4861722624 | bytes 22020096 | tf_op jit(solution)/shard_map/dot_general | solution.py:28
  174.7 15.1 %fusion.6 = bf16[1024,3072]{1,0:T(8,128)(2,1)} fusion(f32[1024,3072]{1,0:T(8,128)} %fusion.53, bf16[1024,768]{1,0:T(8,128)(2,1)S(1)} %bitcast.396, bf16[3072,768]{1,0:T(8,128)(2,1)} %bitcast.381), kind=kOutput, calls=%fused_computation.8 | convolution fusion | flops 4894752768 | bytes 25165824 | tf_op jit(solution)/shard_map/dot_general | solution.py:24
  189.8 7.8 %multiply_reduce_fusion = (bf16[768]{0:T(1024)(128)(2,1)S(1)}, f32[1024]{0:T(1024)S(1)}, f32[1024]{0:T(1024)S(1)}, bf16[768]{0:T(1024)(128)(2,1)S(1)}, f32[1024,768]{1,0:T(8,128)S(1)}) fusion(f32[1024,768]{1,0:T(8,128)S(1)} %get-tuple-element.191, f32[1024]{0:T(1024)S(1)} %add_rsqrt_fusion, f32[1024]{0:T(1024)S(1)} %broadcast_multiply_fusion.4, ...), kind=kOutput, calls=%fused_computation.45 | convolution fusion | flops 4838912000 | bytes 17324032 | tf_op jit(solution)/shard_map/dot_general | solution.py:24
  197.6 2.6 multiply_add_fusion
  200.2 2.6 convolution_convert_fusion.4.grad_ref
  202.8 27.0 %attend_backward.1 = (bf16[1024,768]{1,0:T(8,128)(2,1)S(1)}, bf16[1024,768]{1,0:T(8,128)(2,1)S(1)}, bf16[1024,768]{1,0:T(8,128)(2,1)S(1)}) custom-call(bf16[1024,1920]{1,0:T(8,128)(2,1)} %convolution_convert_fusion.2.q_ref.k_ref.fresh_ref, bf16[1024,1920]{1,0:T(8,128)(2,1)} %convolution_convert_fusion.2.q_ref.k_ref.fresh_ref, ...), custom_call_target="tpu_custom_call" | custom-call | flops 19327352832 | bytes 12582912 | tf_op jit(solution)/shard_map/attend_backward/pallas_call | solution.py:167
  232.0 4.1 fusion.25
  236.2 4.0 convolution_convert_fusion.3
  240.2 2.6 convolution_convert_fusion.5
  242.8 10.2 %convolution_convert_fusion.1 = bf16[768,3072]{1,0:T(8,128)(2,1)} fusion(bf16[1024,3072]{1,0:T(8,128)(2,1)} %fusion.6, f32[1024,768]{1,0:T(8,128)S(1)} %get-tuple-element.191, f32[768]{0:T(1024)S(1)} %get-tuple-element.91, f32[768]{0:T(1024)S(1)} %get-tuple-element.90, f32[1024]{0:T(1024)S(1)} %add_rsqrt_fusion, f32[1024]{0:T(1024)S(1)} %broadcast_multiply_fusion.4), kind=kOutput, calls=%fused_computation.13 | convolution fusion | flops 4838129664 | bytes 14170112 | tf_op jit(solution)/shard_map/dot_general | solution.py:32
  266.7 10.8 %convolution_convert_fusion = bf16[3072,768]{1,0:T(8,128)(2,1)S(1)} fusion(bf16[1024,768]{1,0:T(8,128)(2,1)S(1)} %copy-done.22, f32[1024,3072]{1,0:T(8,128)} %fusion.53), kind=kOutput, calls=%fused_computation.12 | convolution fusion | flops 4862509056 | bytes 18874368 | tf_op jit(solution)/shard_map/dot_general | solution.py:32
  277.6 2.6 constant_dynamic-slice_fusion.3
  283.0 3.1 copy.199
  286.1 3.4 copy.222
  291.1 8.3 %collective-permute-done.30 = bf16[1,512,384]{2,1,0:T(8,128)(2,1)S(1)} collective-permute-done((bf16[1,512,384]{2,1,0:T(8,128)(2,1)}, bf16[1,512,384]{2,1,0:T(8,128)(2,1)S(1)}, u32[]{:S(2)}, u32[]{:S(2)}) %collective-permute-start.30) | collective-permute-done | bytes 393248 | tf_op jit(solution)/shard_map/ppermute | solution.py:208
  306.4 4.7 %copy.185 = bf16[2,2,2,2,24,1024]{4,5,0,1,2,3:T(8,128)(2,1)} copy(bf16[2,2,2,2,24,1024]{5,4,3,2,1,0:T(8,128)(2,1)} %collective-permute-done.31) | data formatting | bytes 1572864 | tf_op jit(solution)/shard_map/ppermute | solution.py:210
  311.1 4.6 %fusion.7 = bf16[2,2,2,2,24,1024]{4,5,0,1,2,3:T(8,128)(2,1)S(1)} fusion(bf16[2,2,2,2,24,1024]{4,5,0,1,2,3:T(8,128)(2,1)} %copy.185, bf16[2,2,2,1,2,24,1024]{5,6,0,1,2,4,3:T(8,128)(2,1)} %copy.199), kind=kLoop, calls=%fused_computation.11 | loop fusion | flops 1572864 | bytes 2359296 | tf_op jit(solution)/shard_map/convert_element_type | solution.py:236
  328.2 8.3 %collective-permute-done.43 = bf16[2,2,24,768]{3,2,0,1:T(8,128)(2,1)S(1)} collective-permute-done((bf16[2,2,24,768]{3,2,0,1:T(8,128)(2,1)S(1)}, bf16[2,2,24,768]{3,2,0,1:T(8,128)(2,1)S(1)}, u32[]{:S(2)}, u32[]{:S(2)}) %collective-permute-start.43) | collective-permute-done | bytes 147488 | tf_op jit(solution)/shard_map/ppermute | solution.py:210
  346.8 2.6 copy.187
  349.4 2.8 fusion.10
  357.6 2.9 collective-permute-done.33
  366.7 10.9 %collective-permute-done.34 = bf16[2,24,1024]{1,2,0:T(8,128)(2,1)S(1)} collective-permute-done((bf16[2,24,1024]{1,2,0:T(8,128)(2,1)S(1)}, bf16[2,24,1024]{1,2,0:T(8,128)(2,1)S(1)}, u32[]{:S(2)}, u32[]{:S(2)}) %collective-permute-start.34) | collective-permute-done | bytes 98336 | tf_op jit(solution)/shard_map/ppermute | solution.py:210
  380.9 7.6 %collective-permute-done.35 = bf16[24,1024]{0,1:T(8,128)(2,1)S(1)} collective-permute-done((bf16[24,1024]{0,1:T(8,128)(2,1)S(1)}, bf16[24,1024]{0,1:T(8,128)(2,1)S(1)}, u32[]{:S(2)}, u32[]{:S(2)}) %collective-permute-start.35) | collective-permute-done | bytes 49184 | tf_op jit(solution)/shard_map/ppermute | solution.py:210
  388.7 3.3 fusion.9
  397.0 16.5 %collective-permute-done.47 = bf16[2,2,2,24,3072]{4,3,0,1,2:T(8,128)(2,1)S(1)} collective-permute-done((bf16[2,2,2,24,3072]{4,3,0,1,2:T(8,128)(2,1)S(1)}, bf16[2,2,2,24,3072]{4,3,0,1,2:T(8,128)(2,1)S(1)}, u32[]{:S(2)}, u32[]{:S(2)}) %collective-permute-start.47) | collective-permute-done | bytes 1179680 | tf_op jit(solution)/shard_map/ppermute | solution.py:208
  415.3 4.2 collective-permute-done.52
  420.9 4.9 %collective-permute-done.48 = bf16[2,2,24,3072]{3,2,0,1:T(8,128)(2,1)S(1)} collective-permute-done((bf16[2,2,24,3072]{3,2,0,1:T(8,128)(2,1)S(1)}, bf16[2,2,24,3072]{3,2,0,1:T(8,128)(2,1)S(1)}, u32[]{:S(2)}, u32[]{:S(2)}) %collective-permute-start.48) | collective-permute-done | bytes 589856 | tf_op jit(solution)/shard_map/ppermute | solution.py:210
  426.0 2.5 collective-permute-start.49
  430.0 2.5 collective-permute-start.54
  432.5 2.6 collective-permute-done.49
  440.0 2.7 collective-permute-done.50
  (365 shorter events, 139.7 us)
Async XLA Ops:
  2.4 19.6 %collective-permute-start.6 = (bf16[24,1024]{1,0:T(8,128)(2,1)}, bf16[24,1024]{1,0:T(8,128)(2,1)}, u32[]{:S(2)}, u32[]{:S(2)}) collective-permute-start(bf16[24,1024]{1,0:T(8,128)(2,1)} %slice.61), channel_id=1, source_target_pairs={{0,16},{2,18},{4,20},{6,22},{8,24},{10,26},{12,28},{14,30},{16,0},... | collective-permute-start | bytes 147464 | tf_op jit(solution)/shard_map/ppermute | solution.py:210
  7.6 75.3 %collective-permute-start = (bf16[1,512,768]{2,1,0:T(8,128)(2,1)S(1)}, bf16[1,512,768]{2,1,0:T(8,128)(2,1)}, u32[]{:S(2)}, u32[]{:S(2)}) collective-permute-start(bf16[1,512,768]{2,1,0:T(8,128)(2,1)S(1)} %constant_dynamic-slice_fusion.11), channel_id=1, source_target_pairs={{0,1},{1,0},{2,3},{3,2},{4,5},{5,4},{6,7},{7,6},{8,9},{9,8},{10,11... | collective-permute-start | bytes 2359304 | tf_op jit(solution)/shard_map/ppermute | solution.py:208
  11.0 47.4 %collective-permute-start.11 = (bf16[1,512,384]{2,1,0:T(8,128)(2,1)}, bf16[1,512,384]{2,1,0:T(8,128)(2,1)S(1)}, u32[]{:S(2)}, u32[]{:S(2)}) collective-permute-start(bf16[1,512,384]{2,1,0:T(8,128)(2,1)} %constant_dynamic-slice_fusion.10), channel_id=1, source_target_pairs={{0,1},{1,0},{2,3},{3,2},{4,5},{5,4},{6,7},{7,6},{8,9},{9,8},{10,11... | collective-permute-start | bytes 1179656 | tf_op jit(solution)/shard_map/ppermute | solution.py:208
  11.5 9.7 %collective-permute-start.12 = (bf16[24,768]{1,0:T(8,128)(2,1)S(1)}, bf16[24,768]{1,0:T(8,128)(2,1)}, u32[]{:S(2)}, u32[]{:S(2)}) collective-permute-start(bf16[24,768]{1,0:T(8,128)(2,1)S(1)} %convert_element_type.367), channel_id=1, source_target_pairs={{0,16},{2,18},{4,20},{6,22},{8,24},{10,26},{12,28},{14,30},{16,0},... | collective-permute-start | bytes 110600 | tf_op jit(solution)/shard_map/ppermute | solution.py:210
  12.3 25.5 %collective-permute-start.22 = (bf16[96,768]{1,0:T(8,128)(2,1)}, bf16[96,768]{1,0:T(8,128)(2,1)}, u32[]{:S(2)}, u32[]{:S(2)}) collective-permute-start(bf16[96,768]{1,0:T(8,128)(2,1)} %convert_element_type.371), channel_id=1, source_target_pairs={{0,16},{2,18},{4,20},{6,22},{8,24},{10,26},{12,28},{14,30},{16,0},... | collective-permute-start | bytes 442376 | tf_op jit(solution)/shard_map/ppermute | solution.py:210
  21.2 16.5 %collective-permute-start.17 = (bf16[24,3072]{1,0:T(8,128)(2,1)}, bf16[24,3072]{1,0:T(8,128)(2,1)S(1)}, u32[]{:S(2)}, u32[]{:S(2)}) collective-permute-start(bf16[24,3072]{1,0:T(8,128)(2,1)} %convert_element_type.369), channel_id=1, source_target_pairs={{0,16},{2,18},{4,20},{6,22},{8,24},{10,26},{12,28},{14,30},{16,0},... | collective-permute-start | bytes 442376 | tf_op jit(solution)/shard_map/ppermute | solution.py:210
  22.8 8.9 %collective-permute-start.1 = (bf16[24,1024]{1,0:T(8,128)(2,1)S(1)}, bf16[24,1024]{1,0:T(8,128)(2,1)S(1)}, u32[]{:S(2)}, u32[]{:S(2)}) collective-permute-start(bf16[24,1024]{1,0:T(8,128)(2,1)S(1)} %get-tuple-element.185), channel_id=1, source_target_pairs={{0,16},{2,18},{4,20},{6,22},{8,24},{10,26},{12,28},{14,30},{16,0},... | collective-permute-start | bytes 147464 | tf_op jit(solution)/shard_map/ppermute | solution.py:210
  36.1 49.0 %collective-permute-start.28 = (bf16[1,512,768]{2,1,0:T(8,128)(2,1)}, bf16[1,512,768]{2,1,0:T(8,128)(2,1)S(1)}, u32[]{:S(2)}, u32[]{:S(2)}) collective-permute-start(bf16[1,512,768]{2,1,0:T(8,128)(2,1)} %constant_dynamic-slice_fusion.9), channel_id=1, source_target_pairs={{0,1},{1,0},{2,3},{3,2},{4,5},{5,4},{6,7},{7,6},{8,9},{9,8},{10,11... | collective-permute-start | bytes 2359304 | tf_op jit(solution)/shard_map/ppermute | solution.py:208
  37.8 6.1 %collective-permute-start.2 = (bf16[2,24,1024]{2,1,0:T(8,128)(2,1)S(1)}, bf16[2,24,1024]{2,1,0:T(8,128)(2,1)S(1)}, u32[]{:S(2)}, u32[]{:S(2)}) collective-permute-start(bf16[2,24,1024]{2,1,0:T(8,128)(2,1)S(1)} %pad_maximum_fusion.35), channel_id=1, source_target_pairs={{0,8},{2,10},{4,12},{6,14},{8,0},{10,2},{12,4},{14,6},{16,24},{18,... | collective-permute-start | bytes 294920 | tf_op jit(solution)/shard_map/ppermute | solution.py:210
  43.9 14.1 %collective-permute-start.8 = (bf16[2,2,24,1024]{3,2,1,0:T(8,128)(2,1)S(1)}, bf16[2,2,24,1024]{3,2,1,0:T(8,128)(2,1)S(1)}, u32[]{:S(2)}, u32[]{:S(2)}) collective-permute-start(bf16[2,2,24,1024]{3,2,1,0:T(8,128)(2,1)S(1)} %pad_maximum_fusion.32), channel_id=1, source_target_pairs={{0,1},{1,0},{2,3},{3,2},{4,5},{5,4},{6,7},{7,6},{8,9},{9,8},{10,11... | collective-permute-start | bytes 589832 | tf_op jit(solution)/shard_map/ppermute | solution.py:208
  47.5 20.8 %collective-permute-start.23 = (bf16[2,96,768]{2,1,0:T(8,128)(2,1)S(1)}, bf16[2,96,768]{2,1,0:T(8,128)(2,1)S(1)}, u32[]{:S(2)}, u32[]{:S(2)}) collective-permute-start(bf16[2,96,768]{2,1,0:T(8,128)(2,1)S(1)} %pad_maximum_fusion.30), channel_id=1, source_target_pairs={{0,8},{2,10},{4,12},{6,14},{8,0},{10,2},{12,4},{14,6},{16,24},{18,... | collective-permute-start | bytes 884744 | tf_op jit(solution)/shard_map/ppermute | solution.py:210
  58.1 8.6 %collective-permute-start.18 = (bf16[2,24,3072]{2,1,0:T(8,128)(2,1)S(1)}, bf16[2,24,3072]{2,1,0:T(8,128)(2,1)S(1)}, u32[]{:S(2)}, u32[]{:S(2)}) collective-permute-start(bf16[2,24,3072]{2,1,0:T(8,128)(2,1)S(1)} %pad_maximum_fusion.29), channel_id=1, source_target_pairs={{0,8},{2,10},{4,12},{6,14},{8,0},{10,2},{12,4},{14,6},{16,24},{18,... | collective-permute-start | bytes 884744 | tf_op jit(solution)/shard_map/ppermute | solution.py:210
  64.2 10.2 %collective-permute-start.15 = (bf16[2,2,2,24,768]{4,3,2,1,0:T(8,128)(2,1)S(1)}, bf16[2,2,2,24,768]{4,3,2,1,0:T(8,128)(2,1)S(1)}, u32[]{:S(2)}, u32[]{:S(2)}) collective-permute-start(bf16[2,2,2,24,768]{4,3,2,1,0:T(8,128)(2,1)S(1)} %pad_maximum_fusion.28), channel_id=1, source_target_pairs={{0,1},{1,0},{2,3},{3,2},{4,5},{5,4},{6,7},{7,6},{8,9},{9,8},{10,11... | collective-permute-start | bytes 884744 | tf_op jit(solution)/shard_map/ppermute | solution.py:208
  66.6 11.1 %collective-permute-start.9 = (bf16[2,2,2,24,1024]{4,3,2,1,0:T(8,128)(2,1)S(1)}, bf16[2,2,2,24,1024]{4,3,2,1,0:T(8,128)(2,1)S(1)}, u32[]{:S(2)}, u32[]{:S(2)}) collective-permute-start(bf16[2,2,2,24,1024]{4,3,2,1,0:T(8,128)(2,1)S(1)} %pad_maximum_fusion.27), channel_id=1, source_target_pairs={{0,4},{2,6},{4,0},{6,2},{8,12},{10,14},{12,8},{14,10},{16,20},{18,... | collective-permute-start | bytes 1179656 | tf_op jit(solution)/shard_map/ppermute | solution.py:210
  68.3 14.5 %collective-permute-start.4 = (bf16[2,2,2,24,1024]{4,3,0,1,2:T(8,128)(2,1)S(1)}, bf16[2,2,2,24,1024]{4,3,0,1,2:T(8,128)(2,1)S(1)}, u32[]{:S(2)}, u32[]{:S(2)}) collective-permute-start(bf16[2,2,2,24,1024]{4,3,0,1,2:T(8,128)(2,1)S(1)} %pad_maximum_fusion.26), channel_id=1, source_target_pairs={{0,1},{1,0},{2,3},{3,2},{4,5},{5,4},{6,7},{7,6},{8,9},{9,8},{10,11... | collective-permute-start | bytes 1179656 | tf_op jit(solution)/shard_map/ppermute | solution.py:208
  74.4 15.8 %collective-permute-start.24 = (bf16[2,2,96,768]{3,2,1,0:T(8,128)(2,1)S(1)}, bf16[2,2,96,768]{3,2,1,0:T(8,128)(2,1)S(1)}, u32[]{:S(2)}, u32[]{:S(2)}) collective-permute-start(bf16[2,2,96,768]{3,2,1,0:T(8,128)(2,1)S(1)} %pad_maximum_fusion.25), channel_id=1, source_target_pairs={{0,1},{1,0},{2,3},{3,2},{4,5},{5,4},{6,7},{7,6},{8,9},{9,8},{10,11... | collective-permute-start | bytes 1769480 | tf_op jit(solution)/shard_map/ppermute | solution.py:208
  77.7 14.2 %collective-permute-start.19 = (bf16[2,2,24,3072]{3,2,1,0:T(8,128)(2,1)S(1)}, bf16[2,2,24,3072]{3,2,1,0:T(8,128)(2,1)S(1)}, u32[]{:S(2)}, u32[]{:S(2)}) collective-permute-start(bf16[2,2,24,3072]{3,2,1,0:T(8,128)(2,1)S(1)} %pad_maximum_fusion.24), channel_id=1, source_target_pairs={{0,4},{2,6},{4,0},{6,2},{8,12},{10,14},{12,8},{14,10},{16,20},{18,... | collective-permute-start | bytes 1769480 | tf_op jit(solution)/shard_map/ppermute | solution.py:210
  82.8 10.9 %collective-permute-start.16 = (bf16[2,2,2,2,24,768]{5,4,3,2,1,0:T(8,128)(2,1)S(1)}, bf16[2,2,2,2,24,768]{5,4,3,2,1,0:T(8,128)(2,1)S(1)}, u32[]{:S(2)}, u32[]{:S(2)}) collective-permute-start(bf16[2,2,2,2,24,768]{5,4,3,2,1,0:T(8,128)(2,1)S(1)} %pad_maximum_fusion.23), channel_id=1, source_target_pairs={{0,2},{2,0},{4,6},{6,4},{8,10},{10,8},{12,14},{14,12},{16,18},{18,... | collective-permute-start | bytes 1769480 | tf_op jit(solution)/shard_map/ppermute | solution.py:210
  83.0 11.9 %collective-permute-start.10 = (bf16[2,2,2,2,24,1024]{5,4,3,2,1,0:T(8,128)(2,1)S(1)}, bf16[2,2,2,2,24,1024]{5,4,3,2,1,0:T(8,128)(2,1)S(1)}, u32[]{:S(2)}, u32[]{:S(2)}) collective-permute-start(bf16[2,2,2,2,24,1024]{5,4,3,2,1,0:T(8,128)(2,1)S(1)} %pad_maximum_fusion.20), channel_id=1, source_target_pairs={{0,2},{2,0},{4,6},{6,4},{8,10},{10,8},{12,14},{14,12},{16,18},{18,... | collective-permute-start | bytes 2359304 | tf_op jit(solution)/shard_map/ppermute | solution.py:210
  85.1 10.3 %collective-permute-start.5 = (bf16[2,2,2,2,24,1024]{5,4,3,2,1,0:T(8,128)(2,1)S(1)}, bf16[2,2,2,2,24,1024]{5,4,3,2,1,0:T(8,128)(2,1)S(1)}, u32[]{:S(2)}, u32[]{:S(2)}) collective-permute-start(bf16[2,2,2,2,24,1024]{5,4,3,2,1,0:T(8,128)(2,1)S(1)} %copy.198), channel_id=1, source_target_pairs={{0,2},{2,0},{4,6},{6,4},{8,10},{10,8},{12,14},{14,12},{16,18},{18,... | collective-permute-start | bytes 2359304 | tf_op jit(solution)/shard_map/ppermute | solution.py:210
  90.4 26.9 %collective-permute-start.25 = (bf16[2,2,2,96,768]{4,3,2,1,0:T(8,128)(2,1)S(1)}, bf16[2,2,2,96,768]{4,3,2,1,0:T(8,128)(2,1)S(1)}, u32[]{:S(2)}, u32[]{:S(2)}) collective-permute-start(bf16[2,2,2,96,768]{4,3,2,1,0:T(8,128)(2,1)S(1)} %pad_maximum_fusion.18), channel_id=1, source_target_pairs={{0,4},{2,6},{4,0},{6,2},{8,12},{10,14},{12,8},{14,10},{16,20},{18,... | collective-permute-start | bytes 3538952 | tf_op jit(solution)/shard_map/ppermute | solution.py:210
  92.1 26.9 %collective-permute-start.20 = (bf16[2,2,2,24,3072]{4,3,2,1,0:T(8,128)(2,1)S(1)}, bf16[2,2,2,24,3072]{4,3,2,1,0:T(8,128)(2,1)S(1)}, u32[]{:S(2)}, u32[]{:S(2)}) collective-permute-start(bf16[2,2,2,24,3072]{4,3,2,1,0:T(8,128)(2,1)S(1)} %pad_maximum_fusion.17), channel_id=1, source_target_pairs={{0,1},{1,0},{2,3},{3,2},{4,5},{5,4},{6,7},{7,6},{8,9},{9,8},{10,11... | collective-permute-start | bytes 3538952 | tf_op jit(solution)/shard_map/ppermute | solution.py:208
  117.7 25.8 %collective-permute-start.26 = (bf16[2,2,2,2,96,768]{5,4,3,2,1,0:T(8,128)(2,1)S(1)}, bf16[2,2,2,2,96,768]{5,4,3,2,1,0:T(8,128)(2,1)}, u32[]{:S(2)}, u32[]{:S(2)}) collective-permute-start(bf16[2,2,2,2,96,768]{5,4,3,2,1,0:T(8,128)(2,1)S(1)} %pad_maximum_fusion.5), channel_id=1, source_target_pairs={{0,2},{2,0},{4,6},{6,4},{8,10},{10,8},{12,14},{14,12},{16,18},{18,... | collective-permute-start | bytes 7077896 | tf_op jit(solution)/shard_map/ppermute | solution.py:210
  120.9 25.0 %collective-permute-start.21 = (bf16[2,2,2,2,24,3072]{5,4,3,2,1,0:T(8,128)(2,1)}, bf16[2,2,2,2,24,3072]{5,4,3,2,1,0:T(8,128)(2,1)}, u32[]{:S(2)}, u32[]{:S(2)}) collective-permute-start(bf16[2,2,2,2,24,3072]{5,4,3,2,1,0:T(8,128)(2,1)} %pad_maximum_fusion.4), channel_id=1, source_target_pairs={{0,2},{2,0},{4,6},{6,4},{8,10},{10,8},{12,14},{14,12},{16,18},{18,... | collective-permute-start | bytes 7077896 | tf_op jit(solution)/shard_map/ppermute | solution.py:210
  253.9 68.0 %collective-permute-start.27 = (bf16[1,512,768]{2,1,0:T(8,128)(2,1)}, bf16[1,512,768]{2,1,0:T(8,128)(2,1)}, u32[]{:S(2)}, u32[]{:S(2)}) collective-permute-start(bf16[1,512,768]{2,1,0:T(8,128)(2,1)} %dynamic-slice_bitcast_fusion.5), channel_id=1, source_target_pairs={{0,1},{1,0},{2,3},{3,2},{4,5},{5,4},{6,7},{7,6},{8,9},{9,8},{10,11... | collective-permute-start | bytes 2359304 | tf_op jit(solution)/shard_map/ppermute | solution.py:208
  259.5 65.9 %collective-permute-start.29 = (bf16[1,512,768]{2,1,0:T(8,128)(2,1)}, bf16[1,512,768]{2,1,0:T(8,128)(2,1)}, u32[]{:S(2)}, u32[]{:S(2)}) collective-permute-start(bf16[1,512,768]{2,1,0:T(8,128)(2,1)} %dynamic-slice_bitcast_fusion.4), channel_id=1, source_target_pairs={{0,1},{1,0},{2,3},{3,2},{4,5},{5,4},{6,7},{7,6},{8,9},{9,8},{10,11... | collective-permute-start | bytes 2359304 | tf_op jit(solution)/shard_map/ppermute | solution.py:208
  260.6 38.8 %collective-permute-start.30 = (bf16[1,512,384]{2,1,0:T(8,128)(2,1)}, bf16[1,512,384]{2,1,0:T(8,128)(2,1)S(1)}, u32[]{:S(2)}, u32[]{:S(2)}) collective-permute-start(bf16[1,512,384]{2,1,0:T(8,128)(2,1)} %dynamic-slice_bitcast_fusion.10), channel_id=1, source_target_pairs={{0,1},{1,0},{2,3},{3,2},{4,5},{5,4},{6,7},{7,6},{8,9},{9,8},{10,11... | collective-permute-start | bytes 1179656 | tf_op jit(solution)/shard_map/ppermute | solution.py:208
  263.8 39.2 %collective-permute-start.36 = (bf16[2,2,2,2,24,1024]{5,4,3,2,1,0:T(8,128)(2,1)}, bf16[2,2,2,2,24,1024]{5,4,3,2,1,0:T(8,128)(2,1)}, u32[]{:S(2)}, u32[]{:S(2)}) collective-permute-start(bf16[2,2,2,2,24,1024]{5,4,3,2,1,0:T(8,128)(2,1)} %dynamic-slice_bitcast_fusion.2), channel_id=1, source_target_pairs={{0,2},{2,0},{4,6},{6,4},{8,10},{10,8},{12,14},{14,12},{16,18},{18,... | collective-permute-start | bytes 2359304 | tf_op jit(solution)/shard_map/ppermute | solution.py:210
  266.7 33.7 %collective-permute-start.41 = (bf16[2,2,2,2,24,768]{5,4,0,1,2,3:T(8,128)(2,1)}, bf16[2,2,2,2,24,768]{5,4,0,1,2,3:T(8,128)(2,1)}, u32[]{:S(2)}, u32[]{:S(2)}) collective-permute-start(bf16[2,2,2,2,24,768]{5,4,0,1,2,3:T(8,128)(2,1)} %bitcast.369), channel_id=1, source_target_pairs={{0,2},{2,0},{4,6},{6,4},{8,10},{10,8},{12,14},{14,12},{16,18},{18,... | collective-permute-start | bytes 1769480 | tf_op jit(solution)/shard_map/ppermute | solution.py:210
  300.5 88.3 %collective-permute-start.46 = (bf16[2,2,2,2,24,3072]{5,4,0,1,2,3:T(8,128)(2,1)}, bf16[2,2,2,2,24,3072]{5,4,0,1,2,3:T(8,128)(2,1)}, u32[]{:S(2)}, u32[]{:S(2)}) collective-permute-start(bf16[2,2,2,2,24,3072]{5,4,0,1,2,3:T(8,128)(2,1)} %bitcast.368), channel_id=1, source_target_pairs={{0,2},{2,0},{4,6},{6,4},{8,10},{10,8},{12,14},{14,12},{16,18},{18,... | collective-permute-start | bytes 7077896 | tf_op jit(solution)/shard_map/ppermute | solution.py:210
  303.1 90.9 %collective-permute-start.51 = (bf16[2,2,2,2,96,768]{5,4,0,1,3,2:T(8,128)(2,1)}, bf16[2,2,2,2,96,768]{5,4,0,1,3,2:T(8,128)(2,1)}, u32[]{:S(2)}, u32[]{:S(2)}) collective-permute-start(bf16[2,2,2,2,96,768]{5,4,0,1,3,2:T(8,128)(2,1)} %bitcast.367), channel_id=1, source_target_pairs={{0,2},{2,0},{4,6},{6,4},{8,10},{10,8},{12,14},{14,12},{16,18},{18,... | collective-permute-start | bytes 7077896 | tf_op jit(solution)/shard_map/ppermute | solution.py:210
  304.6 19.4 %collective-permute-start.42 = (bf16[2,2,2,24,768]{4,3,0,1,2:T(8,128)(2,1)}, bf16[2,2,2,24,768]{4,3,0,1,2:T(8,128)(2,1)}, u32[]{:S(2)}, u32[]{:S(2)}) collective-permute-start(bf16[2,2,2,24,768]{4,3,0,1,2:T(8,128)(2,1)} %dynamic-slice_bitcast_fusion.13), channel_id=1, source_target_pairs={{0,1},{1,0},{2,3},{3,2},{4,5},{5,4},{6,7},{7,6},{8,9},{9,8},{10,11... | collective-permute-start | bytes 884744 | tf_op jit(solution)/shard_map/ppermute | solution.py:208
  321.9 33.2 %collective-permute-start.37 = (bf16[2,2,2,24,1024]{4,3,2,1,0:T(8,128)(2,1)}, bf16[2,2,2,24,1024]{4,3,2,1,0:T(8,128)(2,1)}, u32[]{:S(2)}, u32[]{:S(2)}) collective-permute-start(bf16[2,2,2,24,1024]{4,3,2,1,0:T(8,128)(2,1)} %dynamic-slice_bitcast_fusion.9), channel_id=1, source_target_pairs={{0,4},{2,6},{4,0},{6,2},{8,12},{10,14},{12,8},{14,10},{16,20},{18,... | collective-permute-start | bytes 1179656 | tf_op jit(solution)/shard_map/ppermute | solution.py:210
  324.0 22.8 %collective-permute-start.32 = (bf16[2,2,2,24,1024]{4,3,2,1,0:T(8,128)(2,1)S(1)}, bf16[2,2,2,24,1024]{4,3,2,1,0:T(8,128)(2,1)}, u32[]{:S(2)}, u32[]{:S(2)}) collective-permute-start(bf16[2,2,2,24,1024]{4,3,2,1,0:T(8,128)(2,1)S(1)} %bitcast.400), channel_id=1, source_target_pairs={{0,1},{1,0},{2,3},{3,2},{4,5},{5,4},{6,7},{7,6},{8,9},{9,8},{10,11... | collective-permute-start | bytes 1179656 | tf_op jit(solution)/shard_map/ppermute | solution.py:208
  325.4 11.1 %collective-permute-start.43 = (bf16[2,2,24,768]{3,2,0,1:T(8,128)(2,1)S(1)}, bf16[2,2,24,768]{3,2,0,1:T(8,128)(2,1)S(1)}, u32[]{:S(2)}, u32[]{:S(2)}) collective-permute-start(bf16[2,2,24,768]{3,2,0,1:T(8,128)(2,1)S(1)} %dynamic-slice_bitcast_fusion.18), channel_id=1, source_target_pairs={{0,4},{2,6},{4,0},{6,2},{8,12},{10,14},{12,8},{14,10},{16,20},{18,... | collective-permute-start | bytes 442376 | tf_op jit(solution)/shard_map/ppermute | solution.py:210
  357.1 8.5 %collective-permute-start.38 = (bf16[2,2,24,1024]{3,2,1,0:T(8,128)(2,1)}, bf16[2,2,24,1024]{3,2,1,0:T(8,128)(2,1)}, u32[]{:S(2)}, u32[]{:S(2)}) collective-permute-start(bf16[2,2,24,1024]{3,2,1,0:T(8,128)(2,1)} %dynamic-slice_bitcast_fusion.15), channel_id=1, source_target_pairs={{0,1},{1,0},{2,3},{3,2},{4,5},{5,4},{6,7},{7,6},{8,9},{9,8},{10,11... | collective-permute-start | bytes 589832 | tf_op jit(solution)/shard_map/ppermute | solution.py:208
  363.5 14.1 %collective-permute-start.34 = (bf16[2,24,1024]{1,2,0:T(8,128)(2,1)S(1)}, bf16[2,24,1024]{1,2,0:T(8,128)(2,1)S(1)}, u32[]{:S(2)}, u32[]{:S(2)}) collective-permute-start(bf16[2,24,1024]{1,2,0:T(8,128)(2,1)S(1)} %dynamic-slice_bitcast_fusion.8), channel_id=1, source_target_pairs={{0,8},{2,10},{4,12},{6,14},{8,0},{10,2},{12,4},{14,6},{16,24},{18,... | collective-permute-start | bytes 294920 | tf_op jit(solution)/shard_map/ppermute | solution.py:210
  366.6 12.5 %collective-permute-start.39 = (bf16[2,24,1024]{2,1,0:T(8,128)(2,1)S(1)}, bf16[2,24,1024]{2,1,0:T(8,128)(2,1)S(1)}, u32[]{:S(2)}, u32[]{:S(2)}) collective-permute-start(bf16[2,24,1024]{2,1,0:T(8,128)(2,1)S(1)} %dynamic-slice_bitcast_fusion.19), channel_id=1, source_target_pairs={{0,8},{2,10},{4,12},{6,14},{8,0},{10,2},{12,4},{14,6},{16,24},{18,... | collective-permute-start | bytes 294920 | tf_op jit(solution)/shard_map/ppermute | solution.py:210
  377.8 10.7 %collective-permute-start.35 = (bf16[24,1024]{0,1:T(8,128)(2,1)S(1)}, bf16[24,1024]{0,1:T(8,128)(2,1)S(1)}, u32[]{:S(2)}, u32[]{:S(2)}) collective-permute-start(bf16[24,1024]{0,1:T(8,128)(2,1)S(1)} %dynamic-slice_bitcast_fusion.14), channel_id=1, source_target_pairs={{0,16},{2,18},{4,20},{6,22},{8,24},{10,26},{12,28},{14,30},{16,0},... | collective-permute-start | bytes 147464 | tf_op jit(solution)/shard_map/ppermute | solution.py:210
  379.2 13.6 %collective-permute-start.40 = (bf16[24,1024]{1,0:T(8,128)(2,1)S(1)}, bf16[24,1024]{1,0:T(8,128)(2,1)S(1)}, u32[]{:S(2)}, u32[]{:S(2)}) collective-permute-start(bf16[24,1024]{1,0:T(8,128)(2,1)S(1)} %dynamic-slice_bitcast_fusion.21), channel_id=1, source_target_pairs={{0,16},{2,18},{4,20},{6,22},{8,24},{10,26},{12,28},{14,30},{16,0},... | collective-permute-start | bytes 147464 | tf_op jit(solution)/shard_map/ppermute | solution.py:210
  392.1 21.5 %collective-permute-start.47 = (bf16[2,2,2,24,3072]{4,3,0,1,2:T(8,128)(2,1)S(1)}, bf16[2,2,2,24,3072]{4,3,0,1,2:T(8,128)(2,1)S(1)}, u32[]{:S(2)}, u32[]{:S(2)}) collective-permute-start(bf16[2,2,2,24,3072]{4,3,0,1,2:T(8,128)(2,1)S(1)} %dynamic-slice_bitcast_fusion.1), channel_id=1, source_target_pairs={{0,1},{1,0},{2,3},{3,2},{4,5},{5,4},{6,7},{7,6},{8,9},{9,8},{10,11... | collective-permute-start | bytes 3538952 | tf_op jit(solution)/shard_map/ppermute | solution.py:208
  396.4 23.0 %collective-permute-start.52 = (bf16[2,2,2,96,768]{4,3,0,1,2:T(8,128)(2,1)S(1)}, bf16[2,2,2,96,768]{4,3,0,1,2:T(8,128)(2,1)S(1)}, u32[]{:S(2)}, u32[]{:S(2)}) collective-permute-start(bf16[2,2,2,96,768]{4,3,0,1,2:T(8,128)(2,1)S(1)} %dynamic-slice_bitcast_fusion), channel_id=1, source_target_pairs={{0,4},{2,6},{4,0},{6,2},{8,12},{10,14},{12,8},{14,10},{16,20},{18,... | collective-permute-start | bytes 3538952 | tf_op jit(solution)/shard_map/ppermute | solution.py:210
  414.1 11.7 %collective-permute-start.48 = (bf16[2,2,24,3072]{3,2,0,1:T(8,128)(2,1)S(1)}, bf16[2,2,24,3072]{3,2,0,1:T(8,128)(2,1)S(1)}, u32[]{:S(2)}, u32[]{:S(2)}) collective-permute-start(bf16[2,2,24,3072]{3,2,0,1:T(8,128)(2,1)S(1)} %dynamic-slice_bitcast_fusion.7), channel_id=1, source_target_pairs={{0,4},{2,6},{4,0},{6,2},{8,12},{10,14},{12,8},{14,10},{16,20},{18,... | collective-permute-start | bytes 1769480 | tf_op jit(solution)/shard_map/ppermute | solution.py:210
  419.8 9.9 %collective-permute-start.53 = (bf16[2,2,96,768]{3,2,0,1:T(8,128)(2,1)S(1)}, bf16[2,2,96,768]{3,2,0,1:T(8,128)(2,1)S(1)}, u32[]{:S(2)}, u32[]{:S(2)}) collective-permute-start(bf16[2,2,96,768]{3,2,0,1:T(8,128)(2,1)S(1)} %dynamic-slice_bitcast_fusion.6), channel_id=1, source_target_pairs={{0,1},{1,0},{2,3},{3,2},{4,5},{5,4},{6,7},{7,6},{8,9},{9,8},{10,11... | collective-permute-start | bytes 1769480 | tf_op jit(solution)/shard_map/ppermute | solution.py:208
  426.0 9.1 %collective-permute-start.49 = (bf16[2,24,3072]{2,1,0:T(8,128)(2,1)S(1)}, bf16[2,24,3072]{2,1,0:T(8,128)(2,1)S(1)}, u32[]{:S(2)}, u32[]{:S(2)}) collective-permute-start(bf16[2,24,3072]{2,1,0:T(8,128)(2,1)S(1)} %dynamic-slice_bitcast_fusion.12), channel_id=1, source_target_pairs={{0,8},{2,10},{4,12},{6,14},{8,0},{10,2},{12,4},{14,6},{16,24},{18,... | collective-permute-start | bytes 884744 | tf_op jit(solution)/shard_map/ppermute | solution.py:210
  430.0 8.2 %collective-permute-start.54 = (bf16[2,96,768]{2,1,0:T(8,128)(2,1)S(1)}, bf16[2,96,768]{2,1,0:T(8,128)(2,1)S(1)}, u32[]{:S(2)}, u32[]{:S(2)}) collective-permute-start(bf16[2,96,768]{2,1,0:T(8,128)(2,1)S(1)} %dynamic-slice_bitcast_fusion.11), channel_id=1, source_target_pairs={{0,8},{2,10},{4,12},{6,14},{8,0},{10,2},{12,4},{14,6},{16,24},{18,... | collective-permute-start | bytes 884744 | tf_op jit(solution)/shard_map/ppermute | solution.py:210
  435.2 7.5 %collective-permute-start.50 = (bf16[24,3072]{1,0:T(8,128)(2,1)S(1)}, bf16[24,3072]{1,0:T(8,128)(2,1)S(1)}, u32[]{:S(2)}, u32[]{:S(2)}) collective-permute-start(bf16[24,3072]{1,0:T(8,128)(2,1)S(1)} %dynamic-slice_bitcast_fusion.17), channel_id=1, source_target_pairs={{0,16},{2,18},{4,20},{6,22},{8,24},{10,26},{12,28},{14,30},{16,0},... | collective-permute-start | bytes 442376 | tf_op jit(solution)/shard_map/ppermute | solution.py:210
  438.3 7.7 %collective-permute-start.55 = (bf16[96,768]{1,0:T(8,128)(2,1)S(1)}, bf16[96,768]{1,0:T(8,128)(2,1)S(1)}, u32[]{:S(2)}, u32[]{:S(2)}) collective-permute-start(bf16[96,768]{1,0:T(8,128)(2,1)S(1)} %dynamic-slice_bitcast_fusion.16), channel_id=1, source_target_pairs={{0,16},{2,18},{4,20},{6,22},{8,24},{10,26},{12,28},{14,30},{16,0},... | collective-permute-start | bytes 442376 | tf_op jit(solution)/shard_map/ppermute | solution.py:210
  (67 other events, 575.1 us)
